TPU v7x, 512 devices: a whole 4x4x16 slice. The times are simulated.
512 devices in a mesh: surf: 16 (over x, y_lo, core), src: 32 (over z, y_hi).
Axes of the slice: x: 4, y: 4 (y_hi: 2, y_lo: 2; y = y_hi * 2 + y_lo), z: 16, core: 2. Of those that a mesh axis runs over, the one named last changes fastest.
Arguments:
- source_spectrum: bfloat16 [2, 2, 8192, 8192], P(None, None, 'src', 'surf'), may hold values from -6 to 6
- surf_freq: bfloat16 [2, 2, 8192, 2048], P(None, None, 'surf', 'src'), may hold values from -0.0625 to 0.0625
- centers: int32 [256], P('src'), may hold values from 0 to 8191
- counts: int32 [8192], P('surf'), may hold values from 1 to 2048
Outputs:
- multiples: float32 [2, 2, 8192, 2048], P(None, None, 'src', 'surf')
All inputs are finite; a program needn't handle non-finite values.
Results may differ from a plain program's by a relative error of at most 0.00099.
Values may be sent and summed in bfloat16 or wider, within the bound.
No kernel may reach another device: no remote copies, remote signals or barrier semaphores. Data moves between devices by JAX's collectives and lax.ppermute only.
A program may use at most 64 MiB of HBM per device.

v0:
```python
import jax
import jax.numpy as jnp
from jax import lax
from jax.sharding import PartitionSpec as P

BLOCK = 32
APER = 2048
RAMP = 1024


def complex_terms(left_operand, piece, counts):
    width = piece.shape[-1]
    columns = jnp.arange(width, dtype=jnp.int32)
    live = (columns[None, :] < counts[:, None]).astype(piece.dtype)
    right_operand = piece * live
    real_values = jnp.einsum(
        "...sx,...xr->...sr",
        left_operand[..., 0, :, :],
        right_operand[..., 0, :, :],
        preferred_element_type=jnp.float32,
    ) - jnp.einsum(
        "...sx,...xr->...sr",
        left_operand[..., 1, :, :],
        right_operand[..., 1, :, :],
        preferred_element_type=jnp.float32,
    )
    imaginary_values = jnp.einsum(
        "...sx,...xr->...sr",
        left_operand[..., 0, :, :],
        right_operand[..., 1, :, :],
        preferred_element_type=jnp.float32,
    ) + jnp.einsum(
        "...sx,...xr->...sr",
        left_operand[..., 1, :, :],
        right_operand[..., 0, :, :],
        preferred_element_type=jnp.float32,
    )
    return jnp.stack([real_values, imaginary_values], axis=-3)


def shards(source_spectrum, surf_freq, centers, counts):
    local_width = source_spectrum.shape[3]
    first = lax.axis_index("surf") * local_width
    positions = (first + jnp.arange(local_width, dtype=jnp.int32)).astype(jnp.float32)
    center_rows = jnp.repeat(centers, BLOCK, total_repeat_length=source_spectrum.shape[2]).astype(
        jnp.float32
    )
    distance = jnp.abs(positions[None, :] - center_rows[:, None])
    taper = jnp.clip((APER + RAMP - distance) / RAMP, 0.0, 1.0)
    left_operand = (source_spectrum.astype(jnp.float32) * taper[None, None]).astype(jnp.bfloat16)
    terms = complex_terms(
        left_operand, lax.all_gather(surf_freq, "src", axis=3, tiled=True), counts
    )
    return lax.psum_scatter(terms, "surf", scatter_dimension=3, tiled=True)


def solution(mesh):
    in_specs = (P(None, None, "src", "surf"), P(None, None, "surf", "src"), P("src"), P("surf"))
    out_specs = P(None, None, "src", "surf")
    return jax.shard_map(shards, mesh=mesh, in_specs=in_specs, out_specs=out_specs, check_vma=False)
```

profile of v0, /device:TPU:1, one launch (start us, length us, event | category | flops | bytes accessed | tf_op | source)
XLA Modules:
  0.0 358.3 jit_solution(5606541462849887971)
XLA Ops:
  6.5 0.0 all-gather.2.cloned.1.call-start
  6.5 1.9 copy.9
  8.5 0.0 all-gather.2.cloned.1.call-update
  8.5 0.0 reduce-scatter.2.cloned.1.call-start
  8.6 0.8 add_add_fusion.1
  9.3 1.6 fusion.6
  11.0 4.5 %compare_select_fusion.1 = s32[256,1]{0,1:T(1,128)S(1)} fusion(s32[]{:T(128)} %bitcast.5, s32[]{:T(128)} %bitcast.6, s32[]{:T(128)} %bitcast.7, s32[]{:T(128)} %bitcast.8, s32[]{:T(128)} %bitcast.9, s32[]{:T(128)} %bitcast.11, s32[]{:T(128)} %bitcast.10, s32[256,1]{0,1:T(1,128)S(1)} %bitcast.42, s32[256,1]{0,1:T(1,128)S(1)} %bitcast.40), kind=kLoop, calls=%fused_computation.18 | loop fusion | flops 3584 | bytes 3100 | tf_op jit(solution)/shard_map/jit(_take)/gather | solution.py:45
  15.5 1.3 fusion.5
  16.8 0.2 multiply_clamp_fusion
  17.0 1.5 multiply_convert_fusion
  18.4 1.1 fusion
  19.5 181.9 %all-gather.2.cloned.1.call-done = bf16[2,2,512,2048]{2,1,0,3:T(2,128)(2,1)} async-done(((bf16[2,2,512,64]{2,1,0,3:T(2,128)(2,1)}), bf16[2,2,512,2048]{2,1,0,3:T(2,128)(2,1)}) %all-gather.2.cloned.1.call-update) | async-done | bytes 8388624 | tf_op jit(solution)/shard_map/all_gather | solution.py:52
  201.4 21.2 %copy.10 = bf16[2,2,512,2048]{3,2,0,1:T(8,128)(2,1)} copy(bf16[2,2,512,2048]{2,1,0,3:T(2,128)(2,1)} %all-gather.2.cloned.1.call-done) | data formatting | bytes 16777216 | tf_op jit(solution)/shard_map/all_gather | solution.py:52
  222.6 7.4 %broadcast_multiply_fusion = bf16[2,2,512,2048]{3,2,0,1:T(8,128)(2,1)} fusion(bf16[2,2,512,2048]{3,2,0,1:T(8,128)(2,1)} %copy.10, bf16[512,2048]{1,0:T(8,128)(2,1)S(1)} %fusion), kind=kLoop, calls=%fused_computation.5 | loop fusion | flops 4194304 | bytes 18874368 | tf_op jit(solution)/shard_map/mul | solution.py:15
  230.0 0.0 copy-start
  230.0 3.6 %fusion.1 = f32[2,256,2048]{2,1,0:T(8,128)S(1)} fusion(bf16[2,2,512,2048]{3,2,0,1:T(8,128)(2,1)} %broadcast_multiply_fusion, bf16[2,2,256,512]{3,2,0,1:T(8,128)(2,1)S(1)} %multiply_convert_fusion), kind=kOutput, calls=%fused_computation.8 | convolution fusion | flops 1073741824 | bytes 8912896 | tf_op jit(solution)/shard_map/...sx,...xr->...sr/dot_general | solution.py:32
  233.6 1.0 copy-done
  234.6 1.3 fusion.2
  235.9 1.3 add_bitcast_fusion
  237.2 1.3 subtract_bitcast_fusion
  238.5 4.3 %pad_maximum_fusion = f32[2,2,256,2048]{3,2,0,1:T(8,128)} fusion(f32[2,1,256,2048]{3,2,0,1:T(8,128)S(1)} %add_bitcast_fusion, f32[2,1,256,2048]{3,2,0,1:T(8,128)S(1)} %subtract_bitcast_fusion), kind=kLoop, calls=%fused_computation | loop fusion | flops 2097152 | bytes 16777216 | tf_op jit(solution)/shard_map/stack | solution.py:38
  242.8 0.0 reduce-scatter.2.cloned.1.call-update
  242.8 106.8 %reduce-scatter.2.cloned.1.call-done = f32[2,2,256,128]{3,2,0,1:T(8,128)} async-done(((f32[2,2,256,2048]{3,2,0,1:T(8,128)}), f32[2,2,256,128]{3,2,0,1:T(8,128)}) %reduce-scatter.2.cloned.1.call-update) | async-done | bytes 524304 | tf_op jit(solution)/shard_map/reduce_scatter | solution.py:54
  349.6 1.9 copy.11
  (3 shorter events, 0.0 us)
Async XLA Ops:
  6.5 194.9 %all-gather.2.cloned.1.call-start = ((), (), s32[]{:S(2)}) async-start(), calls=%async_computation.1 | async-start | bytes 8650752 | tf_op jit(solution)/shard_map/all_gather | solution.py:52
  8.5 341.1 %reduce-scatter.2.cloned.1.call-start = ((), (), s32[]{:S(2)}) async-start(), calls=%async_computation.2 | async-start | bytes 8912896 | tf_op jit(solution)/shard_map/reduce_scatter | solution.py:54
  230.0 4.6 %copy-start = (bf16[2,2,512,2048]{3,2,0,1:T(8,128)(2,1)S(1)}, bf16[2,2,512,2048]{3,2,0,1:T(8,128)(2,1)}, u32[]{:S(2)}) copy-start(bf16[2,2,512,2048]{3,2,0,1:T(8,128)(2,1)} %broadcast_multiply_fusion) | copy-start | bytes 25165828
Sparse Core Ops, SparseCore 0:
  10.5 190.8 all-gather.1
  242.9 106.6 reduce-scatter.1
where the time goes:
time: 359 us; the launch traced here: 358 us
  waiting for transfers between devices  289 us (81%)
  local copies, waits for them, and re-layouts  27.6 us (8%)
  other arithmetic  21.1 us (6%)
  between operations  13.5 us (4%)
  matrix products  7.38 us (2%)
    all_gather x1, waiting for transfers between devices, shards(): lax.all_gather(surf_freq, 'src', axis=3, tiled=True)  182 us
    reduce_scatter x1, waiting for transfers between devices, shards(): return lax.psum_scatter(terms, 'surf', scatter_dimension=3, tiled=True)  107 us
    all_gather x1, local copies, waits for them, and re-layouts, shards(): lax.all_gather(surf_freq, 'src', axis=3, tiled=True)  21.2 us
    mul x1, other arithmetic, complex_terms(): right_operand = piece * live  7.44 us
  transfers between devices with their start and end apart: 2, of which 2 were waited for; matrix products, arithmetic and copies ran while one was open for 3% of the time, Pallas kernels for 0%

commit v1 on v0

v1 whole, which is shorter than its diff:
```python
import itertools

import jax
import jax.numpy as jnp
from jax import lax
from jax.experimental import pallas as pl
from jax.experimental.pallas import tpu as pltpu
from jax.sharding import PartitionSpec as P

BLOCK = 32
APER = 2048
RAMP = 1024
AXES = ("surf", "src")
NX, NYL, NC, NZ, NH = 4, 2, 2, 16, 2
ROWS = 256
HALF = 512
LANES = 128
COLS = 64
MSG = 272
SHIFT = 31
VMEM_LIMIT = 48 * 1024 * 1024


def flat(x, yl, c, z, h):
    return ((x * NYL + yl) * NC + c) * NZ * NH + z * NH + h


COORDS = list(itertools.product(range(NX), range(NYL), range(NC), range(NZ), range(NH)))


def groups(key):
    found = {}
    for place in COORDS:
        found.setdefault(key(*place), []).append(flat(*place))
    return list(found.values())


CORE_PAIRS = [(flat(*p), flat(p[0], p[1], 1 - p[2], p[3], p[4])) for p in COORDS]
HALF_PAIRS = [(flat(*p), flat(p[0], p[1], p[2], p[3], 1 - p[4])) for p in COORDS]
ALONG_Z = groups(lambda x, yl, c, z, h: (x, yl, c, h))
PLANE_CHIPS = groups(lambda x, yl, c, z, h: (c, z, h))
CORE_HALF = groups(lambda x, yl, c, z, h: (x, yl, z))


def params():
    return pltpu.CompilerParams(vmem_limit_bytes=VMEM_LIMIT)


def prepare_kernel(where, centers, spectrum, surf, counts, keep_a, keep_b, sent):
    core = where[0]
    first = where[1] * HALF
    column0 = where[2] * COLS
    positions = (first + lax.broadcasted_iota(jnp.int32, (1, HALF), 1)).astype(jnp.float32)
    for f, to_send in ((core, False), (1 - core, True)):
        for part in range(2):
            for block in range(ROWS // BLOCK):
                rows = slice(block * BLOCK, (block + 1) * BLOCK)
                distance = jnp.abs(positions - centers[block].astype(jnp.float32))
                taper = jnp.clip((APER + RAMP - distance) / RAMP, 0.0, 1.0)
                values = (spectrum[f, part, rows, :].astype(jnp.float32) * taper).astype(jnp.bfloat16)
                if to_send:
                    for piece in range(HALF // LANES):
                        at = (part * (HALF // LANES) + piece) * ROWS + block * BLOCK
                        sent[at : at + BLOCK, :] = values[:, piece * LANES : (piece + 1) * LANES]
                else:
                    keep_a[part, rows, :] = values
    lane = lax.broadcasted_iota(jnp.int32, (1, LANES), 1)
    column = (column0 + jnp.where(lane < COLS, lane, lane - COLS)).astype(jnp.float32)
    base = 2 * (HALF // LANES) * ROWS
    for piece in range(HALF // LANES):
        rows = slice(piece * LANES, (piece + 1) * LANES)
        own = counts[piece : piece + 1, :].astype(jnp.float32)
        live = column < jnp.transpose(jnp.broadcast_to(own, (LANES, LANES)))
        for f, to_send in ((core, False), (1 - core, True)):
            both = jnp.concatenate(
                [surf[f, 0, rows, :].astype(jnp.float32), surf[f, 1, rows, :].astype(jnp.float32)], axis=1
            )
            both = jnp.where(live, both, 0.0)
            if to_send:
                sent[base + piece * LANES : base + (piece + 1) * LANES, :] = both.astype(jnp.bfloat16)
            else:
                keep_b[rows, :] = both.astype(jnp.bfloat16)


def prepare(where, centers, spectrum, surf, counts):
    vmem = pl.BlockSpec(memory_space=pltpu.VMEM)
    smem = pl.BlockSpec(memory_space=pltpu.SMEM)
    sent_rows = 2 * (HALF // LANES) * ROWS + HALF
    return pl.pallas_call(
        prepare_kernel,
        out_shape=[
            jax.ShapeDtypeStruct((2, ROWS, HALF), jnp.bfloat16),
            jax.ShapeDtypeStruct((HALF, LANES), jnp.bfloat16),
            jax.ShapeDtypeStruct((sent_rows, LANES), jnp.bfloat16),
        ],
        in_specs=[smem, smem, vmem, vmem, vmem],
        out_specs=[vmem, vmem, vmem],
        compiler_params=params(),
        cost_estimate=pl.CostEstimate(flops=4_000_000, bytes_accessed=3_000_000, transcendentals=0),
        name="prepare",
    )(where, centers, spectrum, surf, counts)


def encode(values):
    values = values.astype(jnp.float32)
    size = jnp.abs(values)
    exponent = jnp.floor(jnp.log2(jnp.maximum(size, 2.0**-126)) + 0.002)
    mantissa = jnp.round((size * 2.0**64) * jnp.exp2(-57.0 - exponent))
    down = jnp.clip(-4.0 - exponent, 0.0, 127.0)
    code = jnp.where(values < 0, -mantissa, mantissa) * 128.0 + down
    return jnp.where(size == 0, 0.0, code).astype(jnp.int32).astype(jnp.int16)


def pack_kernel(where, keep_a, keep_b, received, a, code):
    core = where[0]
    mine = pl.multiple_of(core * HALF, HALF)
    other = pl.multiple_of((1 - core) * HALF, HALF)
    a[:, :, pl.ds(mine, HALF)] = keep_a[...]
    for part in range(2):
        for piece in range(HALF // LANES):
            at = (part * (HALF // LANES) + piece) * ROWS
            column = pl.multiple_of(other + piece * LANES, LANES)
            a[part, :, pl.ds(column, LANES)] = received[at : at + ROWS, :]
    base = 2 * (HALF // LANES) * ROWS
    code[pl.ds(mine, HALF), :] = encode(keep_b[...])
    code[pl.ds(other, HALF), :] = encode(received[base : base + HALF, :])


def pack(where, keep_a, keep_b, received):
    vmem = pl.BlockSpec(memory_space=pltpu.VMEM)
    return pl.pallas_call(
        pack_kernel,
        out_shape=[
            jax.ShapeDtypeStruct((2, ROWS, 2 * HALF), jnp.bfloat16),
            jax.ShapeDtypeStruct((2 * HALF, LANES), jnp.int16),
        ],
        in_specs=[pl.BlockSpec(memory_space=pltpu.SMEM), vmem, vmem, vmem],
        out_specs=[vmem, vmem],
        compiler_params=params(),
        cost_estimate=pl.CostEstimate(flops=2_000_000, bytes_accessed=2_500_000, transcendentals=300_000),
        name="pack",
    )(where, keep_a, keep_b, received)


def exponent_of(largest):
    return jnp.floor(jnp.log2(jnp.maximum(largest, 2.0**-100)) + 0.002) + 1.0


def store_scaled(out, values, shift):
    exponent = exponent_of(jnp.max(jnp.abs(values), axis=0, keepdims=True))
    scaled = jnp.clip(jnp.round(values * jnp.exp2(15.0 - exponent)), -32767.0, 32767.0)
    out[:ROWS, :] = scaled.astype(jnp.int32).astype(jnp.int16)
    below = jnp.broadcast_to(exponent - shift, (MSG - ROWS, LANES))
    out[ROWS:, :] = below.astype(jnp.int32).astype(jnp.int16)


def load_scaled(message):
    exponent = message[ROWS:, :].astype(jnp.int32).astype(jnp.float32)[:1, :]
    return message[:ROWS, :].astype(jnp.int32).astype(jnp.float32) * jnp.exp2(exponent - 15.0)


def product_kernel(where, own, partner, gathered, out, a):
    @pl.when(pl.program_id(0) == 0)
    def _():
        half = where[3]
        a[:, pl.ds(pl.multiple_of(half * ROWS, ROWS), ROWS), :] = own[...]
        a[:, pl.ds(pl.multiple_of((1 - half) * ROWS, ROWS), ROWS), :] = partner[...]

    decoded = []
    for block in range(2):
        code = gathered[block].astype(jnp.int32)
        mantissa = lax.shift_right_arithmetic(code, 7).astype(jnp.float32)
        down = jnp.bitwise_and(code, 127).astype(jnp.float32)
        decoded.append((mantissa * jnp.exp2((SHIFT - 11.0) - down)).astype(jnp.bfloat16))
    b = jnp.concatenate(decoded, axis=1)
    straight = jnp.dot(a[0], b, preferred_element_type=jnp.float32)
    crossed = jnp.dot(a[1], b, preferred_element_type=jnp.float32)
    real = lax.broadcasted_iota(jnp.int32, (1, LANES), 1) < COLS
    for block in range(2):
        lanes = slice(block * LANES, (block + 1) * LANES)
        turned = pltpu.roll(crossed[:, lanes], COLS, 1)
        values = straight[:, lanes] + jnp.where(real, -turned, turned)
        for half in range(2):
            store_scaled(out.at[0, block, half], values[half * ROWS : (half + 1) * ROWS], SHIFT)


def product(where, own, partner, gathered):
    k = 2 * HALF
    return pl.pallas_call(
        product_kernel,
        grid=(8,),
        out_shape=jax.ShapeDtypeStruct((8, 2, 2, MSG, LANES), jnp.int16),
        in_specs=[
            pl.BlockSpec(memory_space=pltpu.SMEM),
            pl.BlockSpec((2, ROWS, k), lambda g: (0, 0, 0)),
            pl.BlockSpec((2, ROWS, k), lambda g: (0, 0, 0)),
            pl.BlockSpec((2, k, LANES), lambda g: (g, 0, 0)),
        ],
        out_specs=pl.BlockSpec((1, 2, 2, MSG, LANES), lambda g: (g, 0, 0, 0, 0)),
        scratch_shapes=[pltpu.VMEM((2, 2 * ROWS, k), jnp.bfloat16)],
        compiler_params=params(),
        cost_estimate=pl.CostEstimate(flops=4_300_000_000, bytes_accessed=9_000_000, transcendentals=2_000_000),
        name="product",
    )(where, own, partner, gathered)


def add_kernel(arrived, out):
    total = load_scaled(arrived.at[0, 0, 0])
    for source in range(1, 8):
        total = total + load_scaled(arrived.at[source, 0, 0])
    store_scaled(out.at[0], total, 0)


def add(arrived):
    return pl.pallas_call(
        add_kernel,
        grid=(4,),
        out_shape=jax.ShapeDtypeStruct((4, MSG, LANES), jnp.int16),
        in_specs=[pl.BlockSpec((8, 1, 1, MSG, LANES), lambda g: (0, g // 2, g % 2, 0, 0))],
        out_specs=pl.BlockSpec((1, MSG, LANES), lambda g: (g, 0, 0)),
        compiler_params=params(),
        cost_estimate=pl.CostEstimate(flops=4_000_000, bytes_accessed=3_000_000, transcendentals=0),
        name="add",
    )(arrived)


def finish_kernel(arrived, out):
    real = lax.broadcasted_iota(jnp.int32, (1, LANES), 1) < COLS
    for f in range(2):
        low = load_scaled(arrived.at[2 * f])
        high = load_scaled(arrived.at[2 * f + 1])
        out[f, 0] = jnp.where(real, low, pltpu.roll(high, COLS, 1))
        out[f, 1] = jnp.where(real, pltpu.roll(low, COLS, 1), high)


def finish(arrived):
    vmem = pl.BlockSpec(memory_space=pltpu.VMEM)
    return pl.pallas_call(
        finish_kernel,
        out_shape=jax.ShapeDtypeStruct((2, 2, ROWS, LANES), jnp.float32),
        in_specs=[vmem],
        out_specs=vmem,
        compiler_params=params(),
        cost_estimate=pl.CostEstimate(flops=1_000_000, bytes_accessed=1_000_000, transcendentals=0),
        name="finish",
    )(arrived)


def shards(source_spectrum, surf_freq, centers, counts):
    surf = lax.axis_index("surf")
    src = lax.axis_index("src")
    where = jnp.stack([surf % 2, surf, src, src % 2]).astype(jnp.int32)
    keep_a, keep_b, sent = prepare(where, centers, source_spectrum, surf_freq, counts.reshape(4, LANES))
    received = lax.ppermute(sent, AXES, CORE_PAIRS)
    own, code = pack(where, keep_a, keep_b, received)
    partner = lax.ppermute(own, AXES, HALF_PAIRS)
    gathered = lax.all_gather(code, AXES, axis_index_groups=ALONG_Z, axis=0)
    messages = product(where, own, partner, gathered)
    arrived = lax.all_to_all(messages, AXES, 0, 0, axis_index_groups=PLANE_CHIPS)
    sums = add(arrived)
    last = lax.all_to_all(sums, AXES, 0, 0, axis_index_groups=CORE_HALF)
    return finish(last)


def solution(mesh):
    in_specs = (P(None, None, "src", "surf"), P(None, None, "surf", "src"), P("src"), P("surf"))
    out_specs = P(None, None, "src", "surf")
    return jax.shard_map(shards, mesh=mesh, in_specs=in_specs, out_specs=out_specs, check_vma=False)
```

time: 359 us -> 133 us (0.37)
  waiting for transfers between devices: 289 us -> 1.7 us
  blocking collectives: 0 us -> 103 us
  local copies, waits for them, and re-layouts: 27.6 us -> 3.78 us
  other arithmetic: 21.1 us -> 0.08 us
  between operations: 13.5 us -> 0.07 us
  Pallas kernels: 0 us -> 13.2 us
  starting transfers between devices: 0.04 us -> 10.7 us
  matrix products: 7.38 us -> 0 us
    all_gather x1 -> x0, waiting for transfers between devices: 182 us -> none  [shards(): lax.all_gather(surf_freq, 'src', axis=3, tiled=True)]
    reduce_scatter x1 -> x0, waiting for transfers between devices: 107 us -> none  [shards(): return lax.psum_scatter(terms, 'surf', scatter_dimension=3, tiled=True)]
    all_gather x0 -> x1, blocking collectives: none -> 60.1 us  [shards(): gathered = lax.all_gather(code, AXES, axis_index_groups=ALONG_Z, axis=0)]
    all_to_all x0 -> x2, blocking collectives: none -> 43.2 us  [the longest x1 23.8 us: shards(): lax.all_to_all(messages, AXES, 0, 0, axis_index_groups=PLANE_CHIPS)]
    all_gather x1 -> x0, local copies, waits for them, and re-layouts: 21.2 us -> none  [shards(): lax.all_gather(surf_freq, 'src', axis=3, tiled=True)]
    pallas_call x0 -> x5, Pallas kernels: none -> 13.2 us  [the longest x1 9.07 us: product(): pl.pallas_call(product_kernel, grid=(8,), out_shape=jax.ShapeDtypeStruct(...]
    ppermute x0 -> x2, starting transfers between devices: none -> 10.7 us  [the longest x1 8.79 us: shards(): received = lax.ppermute(sent, AXES, CORE_PAIRS)]
    mul x1 -> x0, other arithmetic: 7.44 us -> none  [complex_terms(): right_operand = piece * live]
  transfers between devices with their start and end apart: 2 -> 2, of which waited for: 2 -> 1; matrix products, arithmetic and copies ran while one was open for 3% -> 0% of each run, Pallas kernels for 0% -> 0%
where the time goes in v1:
time: 133 us
  blocking collectives  103 us (77%)
  Pallas kernels  13.2 us (10%)
  starting transfers between devices  10.7 us (8%)
  local copies, waits for them, and re-layouts  3.78 us (3%)
  waiting for transfers between devices  1.7 us (1%)
    all_gather x1, blocking collectives, shards(): gathered = lax.all_gather(code, AXES, axis_index_groups=ALONG_Z, axis=0)  60.1 us
    all_to_all x1, blocking collectives, shards(): lax.all_to_all(messages, AXES, 0, 0, axis_index_groups=PLANE_CHIPS)  23.8 us
    all_to_all x1, blocking collectives, shards(): last = lax.all_to_all(sums, AXES, 0, 0, axis_index_groups=CORE_HALF)  19.4 us
    pallas_call x1, Pallas kernels, product(): pl.pallas_call(product_kernel, grid=(8,), out_shape=jax.ShapeDtypeStruct(...  9.07 us
    ppermute x1, starting transfers between devices, shards(): received = lax.ppermute(sent, AXES, CORE_PAIRS)  8.79 us
    unnamed x7, local copies, waits for them, and re-layouts  3.78 us
  transfers between devices with their start and end apart: 2, of which 1 were waited for; matrix products, arithmetic and copies ran while one was open for 0% of the time, Pallas kernels for 0%

profile of v1, /device:TPU:1, one launch (start us, length us, event | category | flops | bytes accessed | tf_op | source)
XLA Modules:
  0.0 132.8 jit_solution(11767871880380412584)
XLA Ops:
  0.0 1.2 copy.5.surf
  1.2 0.1 pad_add_fusion.where
  1.3 0.0 copy-start
  1.3 1.2 copy-done
  2.5 0.0 copy-start.1
  2.6 0.7 copy-done.1
  3.2 0.0 copy-start.2
  3.2 0.7 copy-done.2
  3.9 0.9 prepare.1
  4.8 8.8 %collective-permute-start = (bf16[2560,128]{1,0:T(8,128)(2,1)S(1)}, bf16[2560,128]{1,0:T(8,128)(2,1)S(1)}, u32[]{:S(2)}, u32[]{:S(2)}) collective-permute-start(bf16[2560,128]{1,0:T(8,128)(2,1)S(1)} %get-tuple-element.12), channel_id=1, source_target_pairs={{0,32},{1,33},{2,34},{3,35},{4,36},{5,37},{6,38},{7,39},{8,40},{9,... | collective-permute-start | bytes 1966088 | tf_op jit(solution)/shard_map/ppermute | solution.py:254
  13.6 1.7 %collective-permute-done.received = bf16[2560,128]{1,0:T(8,128)(2,1)S(1)} collective-permute-done((bf16[2560,128]{1,0:T(8,128)(2,1)S(1)}, bf16[2560,128]{1,0:T(8,128)(2,1)S(1)}, u32[]{:S(2)}, u32[]{:S(2)}) %collective-permute-start) | collective-permute-done | bytes 655392 | tf_op jit(solution)/shard_map/ppermute | solution.py:254
  15.3 1.1 pack.1
  16.4 1.9 %collective-permute-start.1 = (bf16[2,256,1024]{2,1,0:T(8,128)(2,1)S(1)}, bf16[2,256,1024]{2,1,0:T(8,128)(2,1)S(1)}, u32[]{:S(2)}, u32[]{:S(2)}) collective-permute-start(bf16[2,256,1024]{2,1,0:T(8,128)(2,1)S(1)} %get-tuple-element.13.own), channel_id=1, source_target_pairs={{0,1},{1,0},{2,3},{3,2},{4,5},{5,4},{6,7},{7,6},{8,9},{9,8},{10,11... | collective-permute-start | bytes 3145736 | tf_op jit(solution)/shard_map/ppermute | solution.py:256
  18.4 60.1 %all-gather.2 = s16[16384,128]{1,0:T(8,128)(2,1)} all-gather(s16[1024,128]{1,0:T(8,128)(2,1)S(1)} %get-tuple-element.14), channel_id=2, replica_groups={{0,2,4,6,8,10,12,14,16,18,20,22,24,26,28,30},{1,3,5,7,9,11,13,15,17,19,..., dimensions={0}, use_global_device_ids=true | all-gather | bytes 4456448 | tf_op jit(solution)/shard_map/all_gather | solution.py:257
  78.5 0.0 collective-permute-done.1.partner
  78.5 9.1 %product.1 = s16[8,2,2,272,128]{4,3,2,1,0:T(8,128)(2,1)S(1)} custom-call(s32[4]{0:T(128)S(1)} %pad_add_fusion.where, bf16[2,256,1024]{2,1,0:T(8,128)(2,1)S(1)} %get-tuple-element.13.own, bf16[2,256,1024]{2,1,0:T(8,128)(2,1)S(1)} %collective-permute-done.1.partner, s16[16,1024,128]{2,1,0:T(8,128)(2,1)} %bitcast.7), custom_call_target="tpu_custom_call" | custom-call | flops 4300000256 | bytes 9000000 | tf_op jit(solution)/shard_map/product/pallas_call | solution.py:189
  87.5 23.8 %all_to_all.10.arrived = s16[8,2,2,272,128]{4,3,2,1,0:T(8,128)(2,1)S(1)} all-to-all(s16[8,2,2,272,128]{4,3,2,1,0:T(8,128)(2,1)S(1)} %product.1), channel_id=1, replica_groups={{0,64,128,192,256,320,384,448},{1,65,129,193,257,321,385,449},{2,66,130..., dimensions={0} | all-to-all | bytes 4456448 | tf_op jit(solution)/shard_map/all_to_all | solution.py:259
  111.3 1.1 add.16
  112.4 19.4 %all_to_all.11.arrived = s16[4,272,128]{2,1,0:T(8,128)(2,1)S(1)} all-to-all(s16[4,272,128]{2,1,0:T(8,128)(2,1)S(1)} %add.16), channel_id=1, replica_groups={{0,1,32,33},{2,3,34,35},{4,5,36,37},{6,7,38,39},{8,9,40,41},{10,11,42,4..., dimensions={0} | all-to-all | bytes 557056 | tf_op jit(solution)/shard_map/all_to_all | solution.py:261
  131.8 1.0 finish.1
Async XLA Ops:
  1.3 1.2 copy-start
  2.5 0.7 copy-start.1
  3.2 0.7 copy-start.2
  4.8 10.5 %collective-permute-start = (bf16[2560,128]{1,0:T(8,128)(2,1)S(1)}, bf16[2560,128]{1,0:T(8,128)(2,1)S(1)}, u32[]{:S(2)}, u32[]{:S(2)}) collective-permute-start(bf16[2560,128]{1,0:T(8,128)(2,1)S(1)} %get-tuple-element.12), channel_id=1, source_target_pairs={{0,32},{1,33},{2,34},{3,35},{4,36},{5,37},{6,38},{7,39},{8,40},{9,... | collective-permute-start | bytes 1966088 | tf_op jit(solution)/shard_map/ppermute | solution.py:254
  16.4 62.0 %collective-permute-start.1 = (bf16[2,256,1024]{2,1,0:T(8,128)(2,1)S(1)}, bf16[2,256,1024]{2,1,0:T(8,128)(2,1)S(1)}, u32[]{:S(2)}, u32[]{:S(2)}) collective-permute-start(bf16[2,256,1024]{2,1,0:T(8,128)(2,1)S(1)} %get-tuple-element.13.own), channel_id=1, source_target_pairs={{0,1},{1,0},{2,3},{3,2},{4,5},{5,4},{6,7},{7,6},{8,9},{9,8},{10,11... | collective-permute-start | bytes 3145736 | tf_op jit(solution)/shard_map/ppermute | solution.py:256

commit v2 on v0

v2 whole, which is shorter than its diff:
```python
import itertools

import jax
import jax.numpy as jnp
from jax import lax
from jax.experimental import pallas as pl
from jax.experimental.pallas import tpu as pltpu
from jax.sharding import PartitionSpec as P

BLOCK = 32
APER = 2048
RAMP = 1024
AXES = ("surf", "src")
NX, NYL, NC, NZ, NH = 4, 2, 2, 16, 2
ROWS = 256
HALF = 512
LANES = 128
COLS = 64
MSG = 272
SHIFT = 31
VMEM_LIMIT = 24 * 1024 * 1024
ALL_VMEM = 62 * 1024 * 1024 + 512 * 1024


def flat(x, yl, c, z, h):
    return ((x * NYL + yl) * NC + c) * NZ * NH + z * NH + h


COORDS = list(itertools.product(range(NX), range(NYL), range(NC), range(NZ), range(NH)))


def groups(key):
    found = {}
    for place in COORDS:
        found.setdefault(key(*place), []).append(flat(*place))
    return list(found.values())


CORE_PAIRS = [(flat(*p), flat(p[0], p[1], 1 - p[2], p[3], p[4])) for p in COORDS]
HALF_PAIRS = [(flat(*p), flat(p[0], p[1], p[2], p[3], 1 - p[4])) for p in COORDS]
ALONG_Z = groups(lambda x, yl, c, z, h: (x, yl, c, h))
PLANE_CHIPS = groups(lambda x, yl, c, z, h: (c, z))


def params(limit=VMEM_LIMIT):
    return pltpu.CompilerParams(vmem_limit_bytes=limit)


def vmem():
    return pl.BlockSpec(memory_space=pltpu.VMEM)


def anywhere():
    return pl.BlockSpec(memory_space=pl.ANY)


def core_index():
    return lax.rem(lax.axis_index("surf"), NC)


def half_index():
    return lax.rem(lax.axis_index("src"), NH)


def prepare_kernel(spectrum_in, surf_in, counts_in, centers_in, keep_a, keep_b, sent, spectrum, surf, counts, centers, sems):
    core = core_index()
    copies = [
        pltpu.make_async_copy(centers_in, centers, sems.at[0]),
        pltpu.make_async_copy(counts_in, counts, sems.at[1]),
        pltpu.make_async_copy(surf_in, surf, sems.at[2]),
        pltpu.make_async_copy(spectrum_in, spectrum, sems.at[3]),
    ]
    for copy in copies:
        copy.start()
    for copy in copies[:3]:
        copy.wait()
    column = lax.axis_index("src") * COLS + lax.broadcasted_iota(jnp.int32, (COLS, LANES), 0)
    for piece in range(HALF // LANES):
        lanes = slice(piece * LANES, (piece + 1) * LANES)
        live = column < counts[piece : piece + 1, :]
        for f, to_send in ((core, False), (1 - core, True)):
            for part in range(2):
                values = jnp.where(live, surf[f, part, :, lanes].astype(jnp.float32), 0.0).astype(jnp.bfloat16)
                if to_send:
                    sent[2 * ROWS + part * COLS : 2 * ROWS + (part + 1) * COLS, lanes] = values
                else:
                    keep_b[part * COLS : (part + 1) * COLS, lanes] = values
    copies[3].wait()
    first = lax.axis_index("surf") * HALF
    positions = (first + lax.broadcasted_iota(jnp.int32, (1, HALF), 1)).astype(jnp.float32)
    for block in range(ROWS // BLOCK):
        rows = slice(block * BLOCK, (block + 1) * BLOCK)
        distance = jnp.abs(positions - centers[block].astype(jnp.float32))
        taper = jnp.clip((APER + RAMP - distance) / RAMP, 0.0, 1.0)
        for part in range(2):
            keep_a[part, rows, :] = (spectrum[core, part, rows, :].astype(jnp.float32) * taper).astype(jnp.bfloat16)
            values = (spectrum[1 - core, part, rows, :].astype(jnp.float32) * taper).astype(jnp.bfloat16)
            sent[part * ROWS + block * BLOCK : part * ROWS + (block + 1) * BLOCK, :] = values


def prepare(spectrum, surf, counts, centers):
    return pl.pallas_call(
        prepare_kernel,
        out_shape=[
            jax.ShapeDtypeStruct((2, ROWS, HALF), jnp.bfloat16),
            jax.ShapeDtypeStruct((2 * COLS, HALF), jnp.bfloat16),
            jax.ShapeDtypeStruct((2 * ROWS + 2 * COLS, HALF), jnp.bfloat16),
        ],
        in_specs=[anywhere()] * 4,
        out_specs=[vmem(), vmem(), vmem()],
        scratch_shapes=[
            pltpu.VMEM((2, 2, ROWS, HALF), jnp.bfloat16),
            pltpu.VMEM((2, 2, COLS, HALF), jnp.bfloat16),
            pltpu.VMEM((HALF // LANES, LANES), jnp.int32),
            pltpu.SMEM((ROWS // BLOCK,), jnp.int32),
            pltpu.SemaphoreType.DMA((4,)),
        ],
        compiler_params=params(ALL_VMEM),
        cost_estimate=pl.CostEstimate(flops=4_000_000, bytes_accessed=3_000_000, transcendentals=0),
        name="prepare",
    )(spectrum, surf, counts, centers)


def encode(values):
    values = values.astype(jnp.float32)
    size = jnp.abs(values)
    exponent = jnp.floor(jnp.log2(jnp.maximum(size, 2.0**-126)) + 0.002)
    mantissa = jnp.round((size * 2.0**64) * jnp.exp2(-57.0 - exponent))
    down = jnp.clip(-4.0 - exponent, 0.0, 127.0)
    code = jnp.where(values < 0, -mantissa, mantissa) * 128.0 + down
    return jnp.where(size == 0, 0.0, code).astype(jnp.int32).astype(jnp.int16)


def pack_kernel(keep_a, keep_b, received, a, code):
    core = core_index()
    mine = pl.multiple_of(core * HALF, HALF)
    other = pl.multiple_of((1 - core) * HALF, HALF)
    code[:, pl.ds(mine, HALF)] = encode(keep_b[...])
    code[:, pl.ds(other, HALF)] = encode(received[2 * ROWS :, :])
    for part in range(2):
        a[:, pl.ds(pl.multiple_of(part * 2 * HALF + mine, HALF), HALF)] = keep_a[part]
        a[:, pl.ds(pl.multiple_of(part * 2 * HALF + other, HALF), HALF)] = received[part * ROWS : (part + 1) * ROWS, :]


def pack(keep_a, keep_b, received):
    return pl.pallas_call(
        pack_kernel,
        out_shape=[
            jax.ShapeDtypeStruct((ROWS, 4 * HALF), jnp.bfloat16),
            jax.ShapeDtypeStruct((2 * COLS, 2 * HALF), jnp.int16),
        ],
        in_specs=[vmem()] * 3,
        out_specs=[vmem()] * 2,
        compiler_params=params(),
        cost_estimate=pl.CostEstimate(flops=2_000_000, bytes_accessed=2_500_000, transcendentals=300_000),
        name="pack",
    )(keep_a, keep_b, received)


def exponent_of(largest):
    return jnp.floor(jnp.log2(jnp.maximum(largest, 2.0**-100)) + 0.002) + 1.0


def store_scaled(out, values, shift):
    exponent = exponent_of(jnp.max(jnp.abs(values), axis=0, keepdims=True))
    scaled = jnp.clip(jnp.round(values * jnp.exp2(15.0 - exponent)), -32767.0, 32767.0)
    out[:ROWS, :] = scaled.astype(jnp.int32).astype(jnp.int16)
    below = jnp.broadcast_to(exponent - shift, (MSG - ROWS, LANES))
    out[ROWS:, :] = below.astype(jnp.int32).astype(jnp.int16)


def load_scaled(message):
    exponent = message[ROWS:, :].astype(jnp.int32).astype(jnp.float32)[:1, :]
    return message[:ROWS, :].astype(jnp.int32).astype(jnp.float32) * jnp.exp2(exponent - 15.0)


def decode_pair(gathered, pair, b):
    k = 2 * HALF
    for block in range(2):
        for part in range(2):
            code = gathered[2 * pair + block, part * COLS : (part + 1) * COLS, :].astype(jnp.int32)
            mantissa = lax.shift_right_arithmetic(code, 7).astype(jnp.float32)
            down = jnp.bitwise_and(code, 127).astype(jnp.float32)
            piece = (mantissa * jnp.exp2((SHIFT - 11.0) - down)).astype(jnp.bfloat16)
            straight = block * LANES + part * COLS
            crossed = block * LANES + (1 - part) * COLS
            b[straight : straight + COLS, :k] = piece
            b[crossed : crossed + COLS, k:] = piece if part == 0 else -piece


def product_kernel(own, partner, gathered, out, a, b_even, b_odd):
    half = half_index()
    a[pl.ds(pl.multiple_of(half * ROWS, ROWS), ROWS), :] = own[...]
    a[pl.ds(pl.multiple_of((1 - half) * ROWS, ROWS), ROWS), :] = partner[...]
    pairs = NZ // 2
    decode_pair(gathered, 0, b_even)
    for pair in range(pairs):
        now, later = (b_even, b_odd) if pair % 2 == 0 else (b_odd, b_even)
        if pair + 1 < pairs:
            decode_pair(gathered, pair + 1, later)
        values = lax.dot_general(a[...], now[...], (((1,), (1,)), ((), ())), preferred_element_type=jnp.float32)
        for half in range(2):
            for core in range(2):
                tile = values[half * ROWS : (half + 1) * ROWS, core * LANES : (core + 1) * LANES]
                store_scaled(out.at[2 * pair + half, core], tile, SHIFT)


def product(own, partner, gathered):
    k = 2 * HALF
    return pl.pallas_call(
        product_kernel,
        out_shape=jax.ShapeDtypeStruct((16, 2, MSG, LANES), jnp.int16),
        in_specs=[vmem()] * 3,
        out_specs=vmem(),
        scratch_shapes=[
            pltpu.VMEM((2 * ROWS, 2 * k), jnp.bfloat16),
            pltpu.VMEM((2 * LANES, 2 * k), jnp.bfloat16),
            pltpu.VMEM((2 * LANES, 2 * k), jnp.bfloat16),
        ],
        compiler_params=params(),
        cost_estimate=pl.CostEstimate(flops=4_300_000_000, bytes_accessed=9_000_000, transcendentals=2_000_000),
        name="product",
    )(own, partner, gathered)


def add_kernel(arrived, keep, sent):
    core = core_index()
    for out, which in ((keep, core), (sent, 1 - core)):
        for half in range(2):
            total = load_scaled(arrived.at[half, which])
            for chip in range(1, 8):
                total = total + load_scaled(arrived.at[2 * chip + half, which])
            out[half] = total


def add(arrived):
    return pl.pallas_call(
        add_kernel,
        out_shape=[jax.ShapeDtypeStruct((2, ROWS, LANES), jnp.float32)] * 2,
        in_specs=[vmem()],
        out_specs=[vmem()] * 2,
        compiler_params=params(),
        cost_estimate=pl.CostEstimate(flops=4_000_000, bytes_accessed=3_000_000, transcendentals=0),
        name="add",
    )(arrived)


def finish_kernel(keep, received, out):
    core = core_index()
    low = lax.broadcasted_iota(jnp.int32, (1, LANES), 1) < COLS
    for values, f in ((keep, core), (received, 1 - core)):
        out[f, 0] = jnp.where(low, values[0], pltpu.roll(values[1], COLS, 1))
        out[f, 1] = jnp.where(low, pltpu.roll(values[0], COLS, 1), values[1])


def finish(keep, received):
    return pl.pallas_call(
        finish_kernel,
        out_shape=jax.ShapeDtypeStruct((2, 2, ROWS, LANES), jnp.float32),
        in_specs=[vmem()] * 2,
        out_specs=vmem(),
        compiler_params=params(),
        cost_estimate=pl.CostEstimate(flops=1_000_000, bytes_accessed=1_000_000, transcendentals=0),
        name="finish",
    )(keep, received)


def shards(source_spectrum, surf_freq, centers, counts):
    surf_t = jnp.swapaxes(surf_freq, 2, 3)
    keep_a, keep_b, sent = prepare(source_spectrum, surf_t, counts.reshape(HALF // LANES, LANES), centers)
    received = lax.ppermute(sent, AXES, CORE_PAIRS)
    own, code = pack(keep_a, keep_b, received)
    partner = lax.ppermute(own, AXES, HALF_PAIRS)
    gathered = lax.all_gather(code, AXES, axis_index_groups=ALONG_Z, axis=0)
    arrived = lax.all_to_all(product(own, partner, gathered), AXES, 0, 0, axis_index_groups=PLANE_CHIPS)
    keep, sent = add(arrived)
    return finish(keep, lax.ppermute(sent, AXES, CORE_PAIRS))


def solution(mesh):
    in_specs = (P(None, None, "src", "surf"), P(None, None, "surf", "src"), P("src"), P("surf"))
    out_specs = P(None, None, "src", "surf")
    return jax.shard_map(shards, mesh=mesh, in_specs=in_specs, out_specs=out_specs, check_vma=False)
```

time: 359 us -> 122 us (0.34)
  waiting for transfers between devices: 289 us -> 3.06 us
  blocking collectives: 0 us -> 86.4 us
  local copies, waits for them, and re-layouts: 27.6 us -> 1.94 us
  other arithmetic: 21.1 us -> 0 us
  starting transfers between devices: 0.04 us -> 20.5 us
  between operations: 13.5 us -> 0.05 us
  Pallas kernels: 0 us -> 10.3 us
  matrix products: 7.38 us -> 0 us
    all_gather x1 -> x0, waiting for transfers between devices: 182 us -> none  [shards(): lax.all_gather(surf_freq, 'src', axis=3, tiled=True)]
    reduce_scatter x1 -> x0, waiting for transfers between devices: 107 us -> none  [shards(): return lax.psum_scatter(terms, 'surf', scatter_dimension=3, tiled=True)]
    all_gather x0 -> x1, blocking collectives: none -> 58.8 us  [shards(): gathered = lax.all_gather(code, AXES, axis_index_groups=ALONG_Z, axis=0)]
    all_to_all x0 -> x1, blocking collectives: none -> 27.6 us  [shards(): lax.all_to_all(product(own, partner, gathered), AXES, 0, 0, axis_index_gr...]
    all_gather x1 -> x0, local copies, waits for them, and re-layouts: 21.2 us -> none  [shards(): lax.all_gather(surf_freq, 'src', axis=3, tiled=True)]
    ppermute x0 -> x3, starting transfers between devices: none -> 20.5 us  [the longest x1 9.75 us: shards(): return finish(keep, lax.ppermute(sent, AXES, CORE_PAIRS))]
    pallas_call x0 -> x5, Pallas kernels: none -> 10.3 us  [the longest x1 5.75 us: product(): pl.pallas_call(product_kernel, out_shape=jax.ShapeDtypeStruct((16, 2, MSG...]
    mul x1 -> x0, other arithmetic: 7.44 us -> none  [complex_terms(): right_operand = piece * live]
  transfers between devices with their start and end apart: 2 -> 3, of which waited for: 2 -> 2; matrix products, arithmetic and copies ran while one was open for 3% -> 0% of each run, Pallas kernels for 0% -> 0%
where the time goes in v2:
time: 122 us
  blocking collectives  86.4 us (71%)
  starting transfers between devices  20.5 us (17%)
  Pallas kernels  10.3 us (8%)
  waiting for transfers between devices  3.06 us (3%)
  local copies, waits for them, and re-layouts  1.94 us (2%)
    all_gather x1, blocking collectives, shards(): gathered = lax.all_gather(code, AXES, axis_index_groups=ALONG_Z, axis=0)  58.8 us
    all_to_all x1, blocking collectives, shards(): lax.all_to_all(product(own, partner, gathered), AXES, 0, 0, axis_index_gr...  27.6 us
    ppermute x1, starting transfers between devices, shards(): return finish(keep, lax.ppermute(sent, AXES, CORE_PAIRS))  9.75 us
    ppermute x1, starting transfers between devices, shards(): received = lax.ppermute(sent, AXES, CORE_PAIRS)  8.79 us
    pallas_call x1, Pallas kernels, product(): pl.pallas_call(product_kernel, out_shape=jax.ShapeDtypeStruct((16, 2, MSG...  5.75 us
    pallas_call x1, Pallas kernels, prepare(): pl.pallas_call(prepare_kernel, out_shape=[jax.ShapeDtypeStruct((2, ROWS,...  2.56 us
  transfers between devices with their start and end apart: 3, of which 2 were waited for; matrix products, arithmetic and copies ran while one was open for 0% of the time, Pallas kernels for 0%

profile of v2, /device:TPU:1, one launch (start us, length us, event | category | flops | bytes accessed | tf_op | source)
XLA Modules:
  0.0 122.1 jit_solution(14044342743666487474)
XLA Ops:
  0.0 2.6 %prepare.1 = (bf16[2,256,512]{2,1,0:T(8,128)(2,1)}, bf16[128,512]{1,0:T(8,128)(2,1)}, bf16[640,512]{1,0:T(8,128)(2,1)}) custom-call(bf16[2,2,256,512]{3,2,1,0:T(8,128)(2,1)} %spectrum_in.1, bf16[2,2,64,512]{3,2,1,0:T(8,128)(2,1)} %bitcast.4, s32[4,128]{1,0:T(4,128)} %bitcast.5, s32[8]{0:T(128)} %centers_in.1), custom_call_target="tpu_custom_call" | custom-call | flops 4000000 | bytes 3000000 | tf_op jit(solution)/shard_map/prepare/pallas_call | solution.py:102
  2.6 8.8 %collective-permute-start = (bf16[640,512]{1,0:T(8,128)(2,1)}, bf16[640,512]{1,0:T(8,128)(2,1)S(1)}, u32[]{:S(2)}, u32[]{:S(2)}) collective-permute-start(bf16[640,512]{1,0:T(8,128)(2,1)} %get-tuple-element.14), channel_id=1, source_target_pairs={{0,32},{1,33},{2,34},{3,35},{4,36},{5,37},{6,38},{7,39},{8,40},{9,... | collective-permute-start | bytes 1966088 | tf_op jit(solution)/shard_map/ppermute | solution.py:271
  11.4 1.9 %collective-permute-done.received = bf16[640,512]{1,0:T(8,128)(2,1)S(1)} collective-permute-done((bf16[640,512]{1,0:T(8,128)(2,1)}, bf16[640,512]{1,0:T(8,128)(2,1)S(1)}, u32[]{:S(2)}, u32[]{:S(2)}) %collective-permute-start) | collective-permute-done | bytes 655392 | tf_op jit(solution)/shard_map/ppermute | solution.py:271
  13.3 0.0 copy-start
  13.3 1.0 copy-done
  14.3 0.0 copy-start.1
  14.3 0.9 copy-done.1
  15.2 0.4 pack.1
  15.6 1.9 %collective-permute-start.1 = (bf16[256,2048]{1,0:T(8,128)(2,1)S(1)}, bf16[256,2048]{1,0:T(8,128)(2,1)S(1)}, u32[]{:S(2)}, u32[]{:S(2)}) collective-permute-start(bf16[256,2048]{1,0:T(8,128)(2,1)S(1)} %get-tuple-element.15.own), channel_id=1, source_target_pairs={{0,1},{1,0},{2,3},{3,2},{4,5},{5,4},{6,7},{7,6},{8,9},{9,8},{10,11... | collective-permute-start | bytes 3145736 | tf_op jit(solution)/shard_map/ppermute | solution.py:273
  17.6 58.8 %all-gather.2 = s16[2048,1024]{1,0:T(8,128)(2,1)S(1)} all-gather(s16[128,1024]{1,0:T(8,128)(2,1)S(1)} %get-tuple-element.16), channel_id=2, replica_groups={{0,2,4,6,8,10,12,14,16,18,20,22,24,26,28,30},{1,3,5,7,9,11,13,15,17,19,..., dimensions={0}, use_global_device_ids=true | all-gather | bytes 4456448 | tf_op jit(solution)/shard_map/all_gather | solution.py:274
  76.3 0.0 collective-permute-done.1.partner
  76.3 5.8 %product.1 = s16[16,2,272,128]{3,2,1,0:T(8,128)(2,1)S(1)} custom-call(bf16[256,2048]{1,0:T(8,128)(2,1)S(1)} %get-tuple-element.15.own, bf16[256,2048]{1,0:T(8,128)(2,1)S(1)} %collective-permute-done.1.partner, s16[16,128,1024]{2,1,0:T(8,128)(2,1)S(1)} %bitcast.3), custom_call_target="tpu_custom_call" | custom-call | flops 4300000256 | bytes 9000000 | tf_op jit(solution)/shard_map/product/pallas_call | solution.py:210
  82.1 27.6 %all_to_all.5.arrived = s16[16,2,272,128]{3,2,1,0:T(8,128)(2,1)S(1)} all-to-all(s16[16,2,272,128]{3,2,1,0:T(8,128)(2,1)S(1)} %product.1), channel_id=1, replica_groups={{0,1,64,65,128,129,192,193,256,257,320,321,384,385,448,449},{2,3,66,67,..., dimensions={0} | all-to-all | bytes 4456448 | tf_op jit(solution)/shard_map/all_to_all | solution.py:275
  109.7 0.6 add.1
  110.2 9.7 %collective-permute-start.2 = (f32[2,256,128]{2,1,0:T(8,128)S(1)}, f32[2,256,128]{2,1,0:T(8,128)S(1)}, u32[]{:S(2)}, u32[]{:S(2)}) collective-permute-start(f32[2,256,128]{2,1,0:T(8,128)S(1)} %get-tuple-element.18), channel_id=1, source_target_pairs={{0,32},{1,33},{2,34},{3,35},{4,36},{5,37},{6,38},{7,39},{8,40},{9,... | collective-permute-start | bytes 786440 | tf_op jit(solution)/shard_map/ppermute | solution.py:277
  120.0 1.1 collective-permute-done.2.received
  121.1 1.0 finish.1
Async XLA Ops:
  2.6 10.7 %collective-permute-start = (bf16[640,512]{1,0:T(8,128)(2,1)}, bf16[640,512]{1,0:T(8,128)(2,1)S(1)}, u32[]{:S(2)}, u32[]{:S(2)}) collective-permute-start(bf16[640,512]{1,0:T(8,128)(2,1)} %get-tuple-element.14), channel_id=1, source_target_pairs={{0,32},{1,33},{2,34},{3,35},{4,36},{5,37},{6,38},{7,39},{8,40},{9,... | collective-permute-start | bytes 1966088 | tf_op jit(solution)/shard_map/ppermute | solution.py:271
  13.3 1.0 copy-start
  14.3 0.9 copy-start.1
  15.6 60.7 %collective-permute-start.1 = (bf16[256,2048]{1,0:T(8,128)(2,1)S(1)}, bf16[256,2048]{1,0:T(8,128)(2,1)S(1)}, u32[]{:S(2)}, u32[]{:S(2)}) collective-permute-start(bf16[256,2048]{1,0:T(8,128)(2,1)S(1)} %get-tuple-element.15.own), channel_id=1, source_target_pairs={{0,1},{1,0},{2,3},{3,2},{4,5},{5,4},{6,7},{7,6},{8,9},{9,8},{10,11... | collective-permute-start | bytes 3145736 | tf_op jit(solution)/shard_map/ppermute | solution.py:273
  110.2 10.9 %collective-permute-start.2 = (f32[2,256,128]{2,1,0:T(8,128)S(1)}, f32[2,256,128]{2,1,0:T(8,128)S(1)}, u32[]{:S(2)}, u32[]{:S(2)}) collective-permute-start(f32[2,256,128]{2,1,0:T(8,128)S(1)} %get-tuple-element.18), channel_id=1, source_target_pairs={{0,32},{1,33},{2,34},{3,35},{4,36},{5,37},{6,38},{7,39},{8,40},{9,... | collective-permute-start | bytes 786440 | tf_op jit(solution)/shard_map/ppermute | solution.py:277

commit v3 on v2

--- a/solution.py
+++ b/solution.py
@@ -1,3 +1,4 @@
+import functools
 import itertools
 
 import jax
@@ -16,7 +17,7 @@
 HALF = 512
 LANES = 128
 COLS = 64
-MSG = 272
+MSG = 528
 SHIFT = 31
 VMEM_LIMIT = 24 * 1024 * 1024
 ALL_VMEM = 62 * 1024 * 1024 + 512 * 1024
@@ -62,13 +63,13 @@
     return lax.rem(lax.axis_index("src"), NH)
 
 
-def prepare_kernel(spectrum_in, surf_in, counts_in, centers_in, keep_a, keep_b, sent, spectrum, surf, counts, centers, sems):
-    core = core_index()
+def prepare_kernel(to_send, spectrum_in, surf_in, counts_in, centers_in, out, spectrum, surf, counts, centers, sems):
+    f = 1 - core_index() if to_send else core_index()
     copies = [
-        pltpu.make_async_copy(centers_in, centers, sems.at[0]),
-        pltpu.make_async_copy(counts_in, counts, sems.at[1]),
-        pltpu.make_async_copy(surf_in, surf, sems.at[2]),
-        pltpu.make_async_copy(spectrum_in, spectrum, sems.at[3]),
+        pltpu.make_async_copy(counts_in, counts, sems.at[0]),
+        pltpu.make_async_copy(centers_in, centers, sems.at[1]),
+        pltpu.make_async_copy(surf_in.at[f], surf, sems.at[2]),
+        pltpu.make_async_copy(spectrum_in.at[f], spectrum, sems.at[3]),
     ]
     for copy in copies:
         copy.start()
@@ -78,13 +79,9 @@
     for piece in range(HALF // LANES):
         lanes = slice(piece * LANES, (piece + 1) * LANES)
         live = column < counts[piece : piece + 1, :]
-        for f, to_send in ((core, False), (1 - core, True)):
-            for part in range(2):
-                values = jnp.where(live, surf[f, part, :, lanes].astype(jnp.float32), 0.0).astype(jnp.bfloat16)
-                if to_send:
-                    sent[2 * ROWS + part * COLS : 2 * ROWS + (part + 1) * COLS, lanes] = values
-                else:
-                    keep_b[part * COLS : (part + 1) * COLS, lanes] = values
+        for part in range(2):
+            values = jnp.where(live, surf[part, :, lanes].astype(jnp.float32), 0.0).astype(jnp.bfloat16)
+            out[2 * ROWS + part * COLS : 2 * ROWS + (part + 1) * COLS, lanes] = values
     copies[3].wait()
     first = lax.axis_index("surf") * HALF
     positions = (first + lax.broadcasted_iota(jnp.int32, (1, HALF), 1)).astype(jnp.float32)
@@ -93,31 +90,26 @@
         distance = jnp.abs(positions - centers[block].astype(jnp.float32))
         taper = jnp.clip((APER + RAMP - distance) / RAMP, 0.0, 1.0)
         for part in range(2):
-            keep_a[part, rows, :] = (spectrum[core, part, rows, :].astype(jnp.float32) * taper).astype(jnp.bfloat16)
-            values = (spectrum[1 - core, part, rows, :].astype(jnp.float32) * taper).astype(jnp.bfloat16)
-            sent[part * ROWS + block * BLOCK : part * ROWS + (block + 1) * BLOCK, :] = values
-
-
-def prepare(spectrum, surf, counts, centers):
-    return pl.pallas_call(
-        prepare_kernel,
-        out_shape=[
-            jax.ShapeDtypeStruct((2, ROWS, HALF), jnp.bfloat16),
-            jax.ShapeDtypeStruct((2 * COLS, HALF), jnp.bfloat16),
-            jax.ShapeDtypeStruct((2 * ROWS + 2 * COLS, HALF), jnp.bfloat16),
-        ],
+            values = (spectrum[part, rows, :].astype(jnp.float32) * taper).astype(jnp.bfloat16)
+            out[part * ROWS + block * BLOCK : part * ROWS + (block + 1) * BLOCK, :] = values
+
+
+def prepare(to_send, spectrum, surf, counts, centers):
+    return pl.pallas_call(
+        functools.partial(prepare_kernel, to_send),
+        out_shape=jax.ShapeDtypeStruct((2 * ROWS + 2 * COLS, HALF), jnp.bfloat16),
         in_specs=[anywhere()] * 4,
-        out_specs=[vmem(), vmem(), vmem()],
+        out_specs=vmem(),
         scratch_shapes=[
-            pltpu.VMEM((2, 2, ROWS, HALF), jnp.bfloat16),
-            pltpu.VMEM((2, 2, COLS, HALF), jnp.bfloat16),
+            pltpu.VMEM((2, ROWS, HALF), jnp.bfloat16),
+            pltpu.VMEM((2, COLS, HALF), jnp.bfloat16),
             pltpu.VMEM((HALF // LANES, LANES), jnp.int32),
             pltpu.SMEM((ROWS // BLOCK,), jnp.int32),
             pltpu.SemaphoreType.DMA((4,)),
         ],
-        compiler_params=params(ALL_VMEM),
-        cost_estimate=pl.CostEstimate(flops=4_000_000, bytes_accessed=3_000_000, transcendentals=0),
-        name="prepare",
+        compiler_params=params(ALL_VMEM if to_send else VMEM_LIMIT),
+        cost_estimate=pl.CostEstimate(flops=2_000_000, bytes_accessed=3_000_000, transcendentals=0),
+        name="prepare_sent" if to_send else "prepare_kept",
     )(spectrum, surf, counts, centers)
 
 
@@ -131,47 +123,51 @@
     return jnp.where(size == 0, 0.0, code).astype(jnp.int32).astype(jnp.int16)
 
 
-def pack_kernel(keep_a, keep_b, received, a, code):
+def pack_kernel(kept, received, a, code):
     core = core_index()
-    mine = pl.multiple_of(core * HALF, HALF)
-    other = pl.multiple_of((1 - core) * HALF, HALF)
-    code[:, pl.ds(mine, HALF)] = encode(keep_b[...])
-    code[:, pl.ds(other, HALF)] = encode(received[2 * ROWS :, :])
-    for part in range(2):
-        a[:, pl.ds(pl.multiple_of(part * 2 * HALF + mine, HALF), HALF)] = keep_a[part]
-        a[:, pl.ds(pl.multiple_of(part * 2 * HALF + other, HALF), HALF)] = received[part * ROWS : (part + 1) * ROWS, :]
-
-
-def pack(keep_a, keep_b, received):
+    for values, which in ((kept, core), (received, 1 - core)):
+        place = pl.multiple_of(which * HALF, HALF)
+        code[:, pl.ds(place, HALF)] = encode(values[2 * ROWS :, :])
+        for part in range(2):
+            columns = pl.ds(pl.multiple_of(part * 2 * HALF + place, HALF), HALF)
+            a[:, columns] = values[part * ROWS : (part + 1) * ROWS, :]
+
+
+def pack(kept, received):
     return pl.pallas_call(
         pack_kernel,
         out_shape=[
             jax.ShapeDtypeStruct((ROWS, 4 * HALF), jnp.bfloat16),
             jax.ShapeDtypeStruct((2 * COLS, 2 * HALF), jnp.int16),
         ],
-        in_specs=[vmem()] * 3,
+        in_specs=[vmem()] * 2,
         out_specs=[vmem()] * 2,
         compiler_params=params(),
         cost_estimate=pl.CostEstimate(flops=2_000_000, bytes_accessed=2_500_000, transcendentals=300_000),
         name="pack",
-    )(keep_a, keep_b, received)
+    )(kept, received)
 
 
 def exponent_of(largest):
     return jnp.floor(jnp.log2(jnp.maximum(largest, 2.0**-100)) + 0.002) + 1.0
 
 
-def store_scaled(out, values, shift):
-    exponent = exponent_of(jnp.max(jnp.abs(values), axis=0, keepdims=True))
-    scaled = jnp.clip(jnp.round(values * jnp.exp2(15.0 - exponent)), -32767.0, 32767.0)
-    out[:ROWS, :] = scaled.astype(jnp.int32).astype(jnp.int16)
-    below = jnp.broadcast_to(exponent - shift, (MSG - ROWS, LANES))
-    out[ROWS:, :] = below.astype(jnp.int32).astype(jnp.int16)
-
-
-def load_scaled(message):
-    exponent = message[ROWS:, :].astype(jnp.int32).astype(jnp.float32)[:1, :]
-    return message[:ROWS, :].astype(jnp.int32).astype(jnp.float32) * jnp.exp2(exponent - 15.0)
+def store_scaled(out, tiles, shift):
+    exponents = []
+    for which, values in enumerate(tiles):
+        exponent = exponent_of(jnp.max(jnp.abs(values), axis=0, keepdims=True))
+        scaled = jnp.clip(jnp.round(values * jnp.exp2(15.0 - exponent)), -32767.0, 32767.0)
+        out[which * ROWS : (which + 1) * ROWS, :] = scaled.astype(jnp.int32).astype(jnp.int16)
+        exponents.append(exponent - shift)
+    row = lax.broadcasted_iota(jnp.int32, (MSG - 2 * ROWS, LANES), 0)
+    out[2 * ROWS :, :] = jnp.where(row == 0, exponents[0], exponents[1]).astype(jnp.int32).astype(jnp.int16)
+
+
+def load_scaled(message, which):
+    below = message[2 * ROWS :, :].astype(jnp.int32).astype(jnp.float32)
+    exponent = jnp.where(which == 0, below[0:1, :], below[1:2, :])
+    values = message[pl.ds(pl.multiple_of(which * ROWS, ROWS), ROWS), :]
+    return values.astype(jnp.int32).astype(jnp.float32) * jnp.exp2(exponent - 15.0)
 
 
 def decode_pair(gathered, pair, b):
@@ -200,16 +196,15 @@
             decode_pair(gathered, pair + 1, later)
         values = lax.dot_general(a[...], now[...], (((1,), (1,)), ((), ())), preferred_element_type=jnp.float32)
         for half in range(2):
-            for core in range(2):
-                tile = values[half * ROWS : (half + 1) * ROWS, core * LANES : (core + 1) * LANES]
-                store_scaled(out.at[2 * pair + half, core], tile, SHIFT)
+            rows = slice(half * ROWS, (half + 1) * ROWS)
+            store_scaled(out.at[2 * pair + half], (values[rows, :LANES], values[rows, LANES:]), SHIFT)
 
 
 def product(own, partner, gathered):
     k = 2 * HALF
     return pl.pallas_call(
         product_kernel,
-        out_shape=jax.ShapeDtypeStruct((16, 2, MSG, LANES), jnp.int16),
+        out_shape=jax.ShapeDtypeStruct((16, MSG, LANES), jnp.int16),
         in_specs=[vmem()] * 3,
         out_specs=vmem(),
         scratch_shapes=[
@@ -227,9 +222,9 @@
     core = core_index()
     for out, which in ((keep, core), (sent, 1 - core)):
         for half in range(2):
-            total = load_scaled(arrived.at[half, which])
+            total = load_scaled(arrived.at[half], which)
             for chip in range(1, 8):
-                total = total + load_scaled(arrived.at[2 * chip + half, which])
+                total = total + load_scaled(arrived.at[2 * chip + half], which)
             out[half] = total
 
 
@@ -267,9 +262,10 @@
 
 def shards(source_spectrum, surf_freq, centers, counts):
     surf_t = jnp.swapaxes(surf_freq, 2, 3)
-    keep_a, keep_b, sent = prepare(source_spectrum, surf_t, counts.reshape(HALF // LANES, LANES), centers)
-    received = lax.ppermute(sent, AXES, CORE_PAIRS)
-    own, code = pack(keep_a, keep_b, received)
+    inputs = (source_spectrum, surf_t, counts.reshape(HALF // LANES, LANES), centers)
+    received = lax.ppermute(prepare(True, *inputs), AXES, CORE_PAIRS)
+    kept = prepare(False, *inputs)
+    own, code = pack(kept, received)
     partner = lax.ppermute(own, AXES, HALF_PAIRS)
     gathered = lax.all_gather(code, AXES, axis_index_groups=ALONG_Z, axis=0)
     arrived = lax.all_to_all(product(own, partner, gathered), AXES, 0, 0, axis_index_groups=PLANE_CHIPS)

time: 122 us -> 120 us (0.984)
  waiting for transfers between devices: 3.06 us -> 1.15 us
    ppermute x1, waiting for transfers between devices: 1.91 us -> 0.01 us  [shards(): received = lax.ppermute(prepare(True, *inputs), AXES, CORE_PAIRS)]
    pallas_call x2 -> x3, Pallas kernels: 8.31 us -> 8.66 us  [the longest x1 5.75 us: product(): pl.pallas_call(product_kernel, out_shape=jax.ShapeDtypeStruct((16, MSG, L...]
  transfers between devices with their start and end apart: 3 -> 3, of which waited for: 2 -> 1; matrix products, arithmetic and copies ran while one was open for 0% -> 0% of each run, Pallas kernels for 0% -> 1%
where the time goes in v3:
time: 120 us
  blocking collectives  85.3 us (71%)
  starting transfers between devices  20.3 us (17%)
  Pallas kernels  10.6 us (9%)
  local copies, waits for them, and re-layouts  2.28 us (2%)
    all_gather x1, blocking collectives, shards(): gathered = lax.all_gather(code, AXES, axis_index_groups=ALONG_Z, axis=0)  58.2 us
    all_to_all x1, blocking collectives, shards(): lax.all_to_all(product(own, partner, gathered), AXES, 0, 0, axis_index_gr...  27.1 us
    ppermute x1, starting transfers between devices, shards(): return finish(keep, lax.ppermute(sent, AXES, CORE_PAIRS))  9.57 us
    ppermute x1, starting transfers between devices, shards(): received = lax.ppermute(prepare(True, *inputs), AXES, CORE_PAIRS)  8.79 us
    pallas_call x1, Pallas kernels, product(): pl.pallas_call(product_kernel, out_shape=jax.ShapeDtypeStruct((16, MSG, L...  5.75 us
    pallas_call x2, Pallas kernels, prepare(): pl.pallas_call(functools.partial(prepare_kernel, to_send), out_shape=jax....  2.92 us
  transfers between devices with their start and end apart: 3, of which 1 were waited for; matrix products, arithmetic and copies ran while one was open for 0% of the time, Pallas kernels for 1%

profile of v3, /device:TPU:1, one launch (start us, length us, event | category | flops | bytes accessed | tf_op | source)
XLA Modules:
  0.0 119.7 jit_solution(13841178291041038392)
XLA Ops:
  0.0 0.0 copy-start
  0.0 2.2 %prepare_sent.1 = bf16[640,512]{1,0:T(8,128)(2,1)} custom-call(bf16[2,2,256,512]{3,2,1,0:T(8,128)(2,1)} %spectrum_in.3, bf16[2,2,64,512]{3,2,1,0:T(8,128)(2,1)} %bitcast.4, s32[4,128]{1,0:T(4,128)} %bitcast.6, s32[8]{0:T(128)} %centers_in.3), custom_call_target="tpu_custom_call" | custom-call | flops 2000000 | bytes 3000000 | tf_op jit(solution)/shard_map/prepare_sent/pallas_call | solution.py:98
  2.2 8.8 %collective-permute-start = (bf16[640,512]{1,0:T(8,128)(2,1)}, bf16[640,512]{1,0:T(8,128)(2,1)S(1)}, u32[]{:S(2)}, u32[]{:S(2)}) collective-permute-start(bf16[640,512]{1,0:T(8,128)(2,1)} %prepare_sent.1), channel_id=1, source_target_pairs={{0,32},{1,33},{2,34},{3,35},{4,36},{5,37},{6,38},{7,39},{8,40},{9,... | collective-permute-start | bytes 1966088 | tf_op jit(solution)/shard_map/ppermute | solution.py:266
  11.0 0.0 copy-done
  11.0 0.0 copy-start.1
  11.0 0.9 copy-done.1
  12.0 0.0 copy-start.2
  12.0 0.7 copy-done.2
  12.6 0.0 copy-start.3
  12.6 0.7 copy-done.3
  13.3 0.7 prepare_kept.1.kept
  14.0 0.0 collective-permute-done.received
  14.0 0.4 pack.1
  14.4 1.9 %collective-permute-start.1 = (bf16[256,2048]{1,0:T(8,128)(2,1)S(1)}, bf16[256,2048]{1,0:T(8,128)(2,1)S(1)}, u32[]{:S(2)}, u32[]{:S(2)}) collective-permute-start(bf16[256,2048]{1,0:T(8,128)(2,1)S(1)} %get-tuple-element.9.own), channel_id=1, source_target_pairs={{0,1},{1,0},{2,3},{3,2},{4,5},{5,4},{6,7},{7,6},{8,9},{9,8},{10,11... | collective-permute-start | bytes 3145736 | tf_op jit(solution)/shard_map/ppermute | solution.py:269
  16.4 58.2 %all-gather.2 = s16[2048,1024]{1,0:T(8,128)(2,1)S(1)} all-gather(s16[128,1024]{1,0:T(8,128)(2,1)S(1)} %get-tuple-element.10), channel_id=2, replica_groups={{0,2,4,6,8,10,12,14,16,18,20,22,24,26,28,30},{1,3,5,7,9,11,13,15,17,19,..., dimensions={0}, use_global_device_ids=true | all-gather | bytes 4456448 | tf_op jit(solution)/shard_map/all_gather | solution.py:270
  74.5 0.0 collective-permute-done.1.partner
  74.5 5.7 %product.1 = s16[16,528,128]{2,1,0:T(8,128)(2,1)S(1)} custom-call(bf16[256,2048]{1,0:T(8,128)(2,1)S(1)} %get-tuple-element.9.own, bf16[256,2048]{1,0:T(8,128)(2,1)S(1)} %collective-permute-done.1.partner, s16[16,128,1024]{2,1,0:T(8,128)(2,1)S(1)} %bitcast.3), custom_call_target="tpu_custom_call" | custom-call | flops 4300000256 | bytes 9000000 | tf_op jit(solution)/shard_map/product/pallas_call | solution.py:205
  80.3 27.1 %all_to_all.5.arrived = s16[16,528,128]{2,1,0:T(8,128)(2,1)S(1)} all-to-all(s16[16,528,128]{2,1,0:T(8,128)(2,1)S(1)} %product.1), channel_id=1, replica_groups={{0,1,64,65,128,129,192,193,256,257,320,321,384,385,448,449},{2,3,66,67,..., dimensions={0} | all-to-all | bytes 4325376 | tf_op jit(solution)/shard_map/all_to_all | solution.py:271
  107.4 0.6 add.1
  108.0 9.6 %collective-permute-start.2 = (f32[2,256,128]{2,1,0:T(8,128)S(1)}, f32[2,256,128]{2,1,0:T(8,128)S(1)}, u32[]{:S(2)}, u32[]{:S(2)}) collective-permute-start(f32[2,256,128]{2,1,0:T(8,128)S(1)} %get-tuple-element.12), channel_id=1, source_target_pairs={{0,32},{1,33},{2,34},{3,35},{4,36},{5,37},{6,38},{7,39},{8,40},{9,... | collective-permute-start | bytes 786440 | tf_op jit(solution)/shard_map/ppermute | solution.py:273
  117.6 1.1 collective-permute-done.2.received
  118.7 1.0 finish.1
Async XLA Ops:
  0.0 11.0 %copy-start = (bf16[2,2,256,512]{3,2,1,0:T(8,128)(2,1)S(1)}, bf16[2,2,256,512]{3,2,1,0:T(8,128)(2,1)}, u32[]{:S(2)}) copy-start(bf16[2,2,256,512]{3,2,1,0:T(8,128)(2,1)} %spectrum_in.3) | copy-start | bytes 3145732
  2.2 11.8 %collective-permute-start = (bf16[640,512]{1,0:T(8,128)(2,1)}, bf16[640,512]{1,0:T(8,128)(2,1)S(1)}, u32[]{:S(2)}, u32[]{:S(2)}) collective-permute-start(bf16[640,512]{1,0:T(8,128)(2,1)} %prepare_sent.1), channel_id=1, source_target_pairs={{0,32},{1,33},{2,34},{3,35},{4,36},{5,37},{6,38},{7,39},{8,40},{9,... | collective-permute-start | bytes 1966088 | tf_op jit(solution)/shard_map/ppermute | solution.py:266
  11.0 1.0 copy-start.1
  12.0 0.7 copy-start.2
  12.6 0.7 copy-start.3
  14.4 60.1 %collective-permute-start.1 = (bf16[256,2048]{1,0:T(8,128)(2,1)S(1)}, bf16[256,2048]{1,0:T(8,128)(2,1)S(1)}, u32[]{:S(2)}, u32[]{:S(2)}) collective-permute-start(bf16[256,2048]{1,0:T(8,128)(2,1)S(1)} %get-tuple-element.9.own), channel_id=1, source_target_pairs={{0,1},{1,0},{2,3},{3,2},{4,5},{5,4},{6,7},{7,6},{8,9},{9,8},{10,11... | collective-permute-start | bytes 3145736 | tf_op jit(solution)/shard_map/ppermute | solution.py:269
  108.0 10.7 %collective-permute-start.2 = (f32[2,256,128]{2,1,0:T(8,128)S(1)}, f32[2,256,128]{2,1,0:T(8,128)S(1)}, u32[]{:S(2)}, u32[]{:S(2)}) collective-permute-start(f32[2,256,128]{2,1,0:T(8,128)S(1)} %get-tuple-element.12), channel_id=1, source_target_pairs={{0,32},{1,33},{2,34},{3,35},{4,36},{5,37},{6,38},{7,39},{8,40},{9,... | collective-permute-start | bytes 786440 | tf_op jit(solution)/shard_map/ppermute | solution.py:273

commit v4 on v3

--- a/solution.py
+++ b/solution.py
@@ -108,7 +108,7 @@
             pltpu.SemaphoreType.DMA((4,)),
         ],
         compiler_params=params(ALL_VMEM if to_send else VMEM_LIMIT),
-        cost_estimate=pl.CostEstimate(flops=2_000_000, bytes_accessed=3_000_000, transcendentals=0),
+        cost_estimate=pl.CostEstimate(flops=2_000_000_000, bytes_accessed=3_000_000, transcendentals=0),
         name="prepare_sent" if to_send else "prepare_kept",
     )(spectrum, surf, counts, centers)
 
@@ -218,25 +218,24 @@
     )(own, partner, gathered)
 
 
-def add_kernel(arrived, keep, sent):
-    core = core_index()
-    for out, which in ((keep, core), (sent, 1 - core)):
-        for half in range(2):
-            total = load_scaled(arrived.at[half], which)
-            for chip in range(1, 8):
-                total = total + load_scaled(arrived.at[2 * chip + half], which)
-            out[half] = total
-
-
-def add(arrived):
-    return pl.pallas_call(
-        add_kernel,
-        out_shape=[jax.ShapeDtypeStruct((2, ROWS, LANES), jnp.float32)] * 2,
+def add_kernel(to_send, arrived, out):
+    which = 1 - core_index() if to_send else core_index()
+    for half in range(2):
+        total = load_scaled(arrived.at[half], which)
+        for chip in range(1, 8):
+            total = total + load_scaled(arrived.at[2 * chip + half], which)
+        out[half] = total
+
+
+def add(to_send, arrived):
+    return pl.pallas_call(
+        functools.partial(add_kernel, to_send),
+        out_shape=jax.ShapeDtypeStruct((2, ROWS, LANES), jnp.float32),
         in_specs=[vmem()],
-        out_specs=[vmem()] * 2,
-        compiler_params=params(),
-        cost_estimate=pl.CostEstimate(flops=4_000_000, bytes_accessed=3_000_000, transcendentals=0),
-        name="add",
+        out_specs=vmem(),
+        compiler_params=params(),
+        cost_estimate=pl.CostEstimate(flops=2_000_000, bytes_accessed=1_500_000, transcendentals=0),
+        name="add_sent" if to_send else "add_kept",
     )(arrived)
 
 
@@ -269,8 +268,8 @@
     partner = lax.ppermute(own, AXES, HALF_PAIRS)
     gathered = lax.all_gather(code, AXES, axis_index_groups=ALONG_Z, axis=0)
     arrived = lax.all_to_all(product(own, partner, gathered), AXES, 0, 0, axis_index_groups=PLANE_CHIPS)
-    keep, sent = add(arrived)
-    return finish(keep, lax.ppermute(sent, AXES, CORE_PAIRS))
+    received = lax.ppermute(add(True, arrived), AXES, CORE_PAIRS)
+    return finish(add(False, arrived), received)
 
 
 def solution(mesh):

time: 120 us -> 119 us (level)
  local copies, waits for them, and re-layouts: 2.28 us -> 0.02 us
    unnamed x8, local copies, waits for them, and re-layouts: 2.28 us -> 0.02 us
  transfers between devices with their start and end apart: 3 -> 3, of which waited for: 1 -> 2; matrix products, arithmetic and copies ran while one was open for 0% -> 0% of each run, Pallas kernels for 1% -> 1%
where the time goes in v4:
time: 119 us
  blocking collectives  85.8 us (72%)
  starting transfers between devices  20.4 us (17%)
  Pallas kernels  10.7 us (9%)
  waiting for transfers between devices  1.97 us (2%)
    all_gather x1, blocking collectives, shards(): gathered = lax.all_gather(code, AXES, axis_index_groups=ALONG_Z, axis=0)  58.8 us
    all_to_all x1, blocking collectives, shards(): lax.all_to_all(product(own, partner, gathered), AXES, 0, 0, axis_index_gr...  27 us
    ppermute x1, starting transfers between devices, shards(): received = lax.ppermute(add(True, arrived), AXES, CORE_PAIRS)  9.71 us
    ppermute x1, starting transfers between devices, shards(): received = lax.ppermute(prepare(True, *inputs), AXES, CORE_PAIRS)  8.78 us
    pallas_call x1, Pallas kernels, product(): pl.pallas_call(product_kernel, out_shape=jax.ShapeDtypeStruct((16, MSG, L...  5.74 us
    pallas_call x2, Pallas kernels, prepare(): pl.pallas_call(functools.partial(prepare_kernel, to_send), out_shape=jax....  2.94 us
  transfers between devices with their start and end apart: 3, of which 2 were waited for; matrix products, arithmetic and copies ran while one was open for 0% of the time, Pallas kernels for 1%

profile of v4, /device:TPU:1, one launch (start us, length us, event | category | flops | bytes accessed | tf_op | source)
XLA Modules:
  0.0 118.9 jit_solution(5434049100828063064)
XLA Ops:
  0.0 0.0 copy-start
  0.0 0.0 copy-start.1
  0.0 0.0 copy-start.2
  0.0 0.0 copy-start.3
  0.0 2.2 %prepare_sent.1 = bf16[640,512]{1,0:T(8,128)(2,1)} custom-call(bf16[2,2,256,512]{3,2,1,0:T(8,128)(2,1)} %spectrum_in.3, bf16[2,2,64,512]{3,2,1,0:T(8,128)(2,1)} %bitcast.4, s32[4,128]{1,0:T(4,128)} %bitcast.6, s32[8]{0:T(128)} %centers_in.3), custom_call_target="tpu_custom_call" | custom-call | flops 2000000000 | bytes 3000000 | tf_op jit(solution)/shard_map/prepare_sent/pallas_call | solution.py:98
  2.2 8.8 %collective-permute-start = (bf16[640,512]{1,0:T(8,128)(2,1)}, bf16[640,512]{1,0:T(8,128)(2,1)S(1)}, u32[]{:S(2)}, u32[]{:S(2)}) collective-permute-start(bf16[640,512]{1,0:T(8,128)(2,1)} %prepare_sent.1), channel_id=1, source_target_pairs={{0,32},{1,33},{2,34},{3,35},{4,36},{5,37},{6,38},{7,39},{8,40},{9,... | collective-permute-start | bytes 1966088 | tf_op jit(solution)/shard_map/ppermute | solution.py:265
  11.0 0.0 copy-done
  11.0 0.0 copy-done.1
  11.0 0.0 copy-done.2
  11.0 0.0 copy-done.3
  11.1 0.7 prepare_kept.1.kept
  11.8 1.1 collective-permute-done.received
  12.9 0.4 pack.1
  13.3 1.9 %collective-permute-start.1 = (bf16[256,2048]{1,0:T(8,128)(2,1)S(1)}, bf16[256,2048]{1,0:T(8,128)(2,1)S(1)}, u32[]{:S(2)}, u32[]{:S(2)}) collective-permute-start(bf16[256,2048]{1,0:T(8,128)(2,1)S(1)} %get-tuple-element.7.own), channel_id=1, source_target_pairs={{0,1},{1,0},{2,3},{3,2},{4,5},{5,4},{6,7},{7,6},{8,9},{9,8},{10,11... | collective-permute-start | bytes 3145736 | tf_op jit(solution)/shard_map/ppermute | solution.py:268
  15.3 58.8 %all-gather.2 = s16[2048,1024]{1,0:T(8,128)(2,1)S(1)} all-gather(s16[128,1024]{1,0:T(8,128)(2,1)S(1)} %get-tuple-element.8), channel_id=2, replica_groups={{0,2,4,6,8,10,12,14,16,18,20,22,24,26,28,30},{1,3,5,7,9,11,13,15,17,19,..., dimensions={0}, use_global_device_ids=true | all-gather | bytes 4456448 | tf_op jit(solution)/shard_map/all_gather | solution.py:269
  74.0 0.0 collective-permute-done.1.partner
  74.0 5.7 %product.1 = s16[16,528,128]{2,1,0:T(8,128)(2,1)S(1)} custom-call(bf16[256,2048]{1,0:T(8,128)(2,1)S(1)} %get-tuple-element.7.own, bf16[256,2048]{1,0:T(8,128)(2,1)S(1)} %collective-permute-done.1.partner, s16[16,128,1024]{2,1,0:T(8,128)(2,1)S(1)} %bitcast.3), custom_call_target="tpu_custom_call" | custom-call | flops 4300000256 | bytes 9000000 | tf_op jit(solution)/shard_map/product/pallas_call | solution.py:205
  79.8 27.0 %all_to_all.5.arrived = s16[16,528,128]{2,1,0:T(8,128)(2,1)S(1)} all-to-all(s16[16,528,128]{2,1,0:T(8,128)(2,1)S(1)} %product.1), channel_id=1, replica_groups={{0,1,64,65,128,129,192,193,256,257,320,321,384,385,448,449},{2,3,66,67,..., dimensions={0} | all-to-all | bytes 4325376 | tf_op jit(solution)/shard_map/all_to_all | solution.py:270
  106.8 0.3 add_sent.1
  107.1 9.7 %collective-permute-start.2 = (f32[2,256,128]{2,1,0:T(8,128)S(1)}, f32[2,256,128]{2,1,0:T(8,128)S(1)}, u32[]{:S(2)}, u32[]{:S(2)}) collective-permute-start(f32[2,256,128]{2,1,0:T(8,128)S(1)} %add_sent.1), channel_id=1, source_target_pairs={{0,32},{1,33},{2,34},{3,35},{4,36},{5,37},{6,38},{7,39},{8,40},{9,... | collective-permute-start | bytes 786440 | tf_op jit(solution)/shard_map/ppermute | solution.py:271
  116.8 0.3 add_kept.1.keep
  117.1 0.8 collective-permute-done.2.received
  117.9 1.0 finish.1
Async XLA Ops:
  0.0 11.0 %copy-start = (bf16[2,2,256,512]{3,2,1,0:T(8,128)(2,1)S(1)}, bf16[2,2,256,512]{3,2,1,0:T(8,128)(2,1)}, u32[]{:S(2)}) copy-start(bf16[2,2,256,512]{3,2,1,0:T(8,128)(2,1)} %spectrum_in.3) | copy-start | bytes 3145732
  0.0 11.0 %copy-start.1 = (bf16[2,2,512,64]{2,3,1,0:T(8,128)(2,1)S(1)}, bf16[2,2,512,64]{2,3,1,0:T(8,128)(2,1)}, u32[]{:S(2)}) copy-start(bf16[2,2,512,64]{2,3,1,0:T(8,128)(2,1)} %param.5) | copy-start | bytes 786436
  0.0 11.0 %copy-start.2 = (s32[512]{0:T(512)S(1)}, s32[512]{0:T(512)}, u32[]{:S(2)}) copy-start(s32[512]{0:T(512)} %param.7) | copy-start | bytes 6148
  0.0 11.0 %copy-start.3 = (s32[8]{0:T(128)S(1)}, s32[8]{0:T(128)}, u32[]{:S(2)}) copy-start(s32[8]{0:T(128)} %centers_in.3) | copy-start | bytes 100
  2.2 10.7 %collective-permute-start = (bf16[640,512]{1,0:T(8,128)(2,1)}, bf16[640,512]{1,0:T(8,128)(2,1)S(1)}, u32[]{:S(2)}, u32[]{:S(2)}) collective-permute-start(bf16[640,512]{1,0:T(8,128)(2,1)} %prepare_sent.1), channel_id=1, source_target_pairs={{0,32},{1,33},{2,34},{3,35},{4,36},{5,37},{6,38},{7,39},{8,40},{9,... | collective-permute-start | bytes 1966088 | tf_op jit(solution)/shard_map/ppermute | solution.py:265
  13.3 60.7 %collective-permute-start.1 = (bf16[256,2048]{1,0:T(8,128)(2,1)S(1)}, bf16[256,2048]{1,0:T(8,128)(2,1)S(1)}, u32[]{:S(2)}, u32[]{:S(2)}) collective-permute-start(bf16[256,2048]{1,0:T(8,128)(2,1)S(1)} %get-tuple-element.7.own), channel_id=1, source_target_pairs={{0,1},{1,0},{2,3},{3,2},{4,5},{5,4},{6,7},{7,6},{8,9},{9,8},{10,11... | collective-permute-start | bytes 3145736 | tf_op jit(solution)/shard_map/ppermute | solution.py:268
  107.1 10.9 %collective-permute-start.2 = (f32[2,256,128]{2,1,0:T(8,128)S(1)}, f32[2,256,128]{2,1,0:T(8,128)S(1)}, u32[]{:S(2)}, u32[]{:S(2)}) collective-permute-start(f32[2,256,128]{2,1,0:T(8,128)S(1)} %add_sent.1), channel_id=1, source_target_pairs={{0,32},{1,33},{2,34},{3,35},{4,36},{5,37},{6,38},{7,39},{8,40},{9,... | collective-permute-start | bytes 786440 | tf_op jit(solution)/shard_map/ppermute | solution.py:271

commit v5 on v4

--- a/solution.py
+++ b/solution.py
@@ -63,35 +63,48 @@
     return lax.rem(lax.axis_index("src"), NH)
 
 
-def prepare_kernel(to_send, spectrum_in, surf_in, counts_in, centers_in, out, spectrum, surf, counts, centers, sems):
+def prepare_kernel(to_send, spectrum_in, surf_in, counts_in, centers_in, out, spectrum, surf, counts, centers, done, sems):
     f = 1 - core_index() if to_send else core_index()
     copies = [
         pltpu.make_async_copy(counts_in, counts, sems.at[0]),
         pltpu.make_async_copy(centers_in, centers, sems.at[1]),
         pltpu.make_async_copy(surf_in.at[f], surf, sems.at[2]),
-        pltpu.make_async_copy(spectrum_in.at[f], spectrum, sems.at[3]),
+        pltpu.make_async_copy(spectrum_in.at[f, 0], spectrum.at[0], sems.at[3]),
+        pltpu.make_async_copy(spectrum_in.at[f, 1], spectrum.at[1], sems.at[4]),
     ]
     for copy in copies:
         copy.start()
     for copy in copies[:3]:
         copy.wait()
+    result = done if to_send else out
+    leaving = []
+
+    def leave(rows):
+        if to_send:
+            leaving.append(pltpu.make_async_copy(done.at[rows], out.at[rows], sems.at[5 + len(leaving)]))
+            leaving[-1].start()
+
     column = lax.axis_index("src") * COLS + lax.broadcasted_iota(jnp.int32, (COLS, LANES), 0)
     for piece in range(HALF // LANES):
         lanes = slice(piece * LANES, (piece + 1) * LANES)
         live = column < counts[piece : piece + 1, :]
         for part in range(2):
             values = jnp.where(live, surf[part, :, lanes].astype(jnp.float32), 0.0).astype(jnp.bfloat16)
-            out[2 * ROWS + part * COLS : 2 * ROWS + (part + 1) * COLS, lanes] = values
-    copies[3].wait()
+            result[2 * ROWS + part * COLS : 2 * ROWS + (part + 1) * COLS, lanes] = values
+    leave(slice(2 * ROWS, 2 * ROWS + 2 * COLS))
     first = lax.axis_index("surf") * HALF
     positions = (first + lax.broadcasted_iota(jnp.int32, (1, HALF), 1)).astype(jnp.float32)
-    for block in range(ROWS // BLOCK):
-        rows = slice(block * BLOCK, (block + 1) * BLOCK)
-        distance = jnp.abs(positions - centers[block].astype(jnp.float32))
-        taper = jnp.clip((APER + RAMP - distance) / RAMP, 0.0, 1.0)
-        for part in range(2):
+    for part in range(2):
+        copies[3 + part].wait()
+        for block in range(ROWS // BLOCK):
+            rows = slice(block * BLOCK, (block + 1) * BLOCK)
+            distance = jnp.abs(positions - centers[block].astype(jnp.float32))
+            taper = jnp.clip((APER + RAMP - distance) / RAMP, 0.0, 1.0)
             values = (spectrum[part, rows, :].astype(jnp.float32) * taper).astype(jnp.bfloat16)
-            out[part * ROWS + block * BLOCK : part * ROWS + (block + 1) * BLOCK, :] = values
+            result[part * ROWS + block * BLOCK : part * ROWS + (block + 1) * BLOCK, :] = values
+        leave(slice(part * ROWS, (part + 1) * ROWS))
+    for copy in leaving:
+        copy.wait()
 
 
 def prepare(to_send, spectrum, surf, counts, centers):
@@ -99,13 +112,14 @@
         functools.partial(prepare_kernel, to_send),
         out_shape=jax.ShapeDtypeStruct((2 * ROWS + 2 * COLS, HALF), jnp.bfloat16),
         in_specs=[anywhere()] * 4,
-        out_specs=vmem(),
+        out_specs=anywhere() if to_send else vmem(),
         scratch_shapes=[
             pltpu.VMEM((2, ROWS, HALF), jnp.bfloat16),
             pltpu.VMEM((2, COLS, HALF), jnp.bfloat16),
             pltpu.VMEM((HALF // LANES, LANES), jnp.int32),
             pltpu.SMEM((ROWS // BLOCK,), jnp.int32),
-            pltpu.SemaphoreType.DMA((4,)),
+            pltpu.VMEM((2 * ROWS + 2 * COLS, HALF), jnp.bfloat16),
+            pltpu.SemaphoreType.DMA((8,)),
         ],
         compiler_params=params(ALL_VMEM if to_send else VMEM_LIMIT),
         cost_estimate=pl.CostEstimate(flops=2_000_000_000, bytes_accessed=3_000_000, transcendentals=0),

time: 119 us -> 119 us (level)
  no operation moved by 1% of the time
where the time goes in v5:
time: 119 us
  blocking collectives  85.8 us (72%)
  starting transfers between devices  20.4 us (17%)
  Pallas kernels  10.6 us (9%)
  waiting for transfers between devices  1.9 us (2%)
    all_gather x1, blocking collectives, shards(): gathered = lax.all_gather(code, AXES, axis_index_groups=ALONG_Z, axis=0)  58.8 us
    all_to_all x1, blocking collectives, shards(): lax.all_to_all(product(own, partner, gathered), AXES, 0, 0, axis_index_gr...  27 us
    ppermute x1, starting transfers between devices, shards(): received = lax.ppermute(add(True, arrived), AXES, CORE_PAIRS)  9.71 us
    ppermute x1, starting transfers between devices, shards(): received = lax.ppermute(prepare(True, *inputs), AXES, CORE_PAIRS)  8.78 us
    pallas_call x1, Pallas kernels, product(): pl.pallas_call(product_kernel, out_shape=jax.ShapeDtypeStruct((16, MSG, L...  5.75 us
    pallas_call x2, Pallas kernels, prepare(): pl.pallas_call(functools.partial(prepare_kernel, to_send), out_shape=jax....  2.86 us
  transfers between devices with their start and end apart: 3, of which 2 were waited for; matrix products, arithmetic and copies ran while one was open for 0% of the time, Pallas kernels for 1%

profile of v5, /device:TPU:1, one launch (start us, length us, event | category | flops | bytes accessed | tf_op | source)
XLA Modules:
  0.0 118.8 jit_solution(4872411939778520299)
XLA Ops:
  0.0 0.0 copy-start
  0.0 0.0 copy-start.1
  0.0 0.0 copy-start.2
  0.0 0.0 copy-start.3
  0.0 2.1 %prepare_sent.1 = bf16[640,512]{1,0:T(8,128)(2,1)} custom-call(bf16[2,2,256,512]{3,2,1,0:T(8,128)(2,1)} %spectrum_in.3, bf16[2,2,64,512]{3,2,1,0:T(8,128)(2,1)} %bitcast.4, s32[4,128]{1,0:T(4,128)} %bitcast.6, s32[8]{0:T(128)} %centers_in.3), custom_call_target="tpu_custom_call" | custom-call | flops 2000000000 | bytes 3000000 | tf_op jit(solution)/shard_map/prepare_sent/pallas_call | solution.py:111
  2.1 8.8 %collective-permute-start = (bf16[640,512]{1,0:T(8,128)(2,1)}, bf16[640,512]{1,0:T(8,128)(2,1)S(1)}, u32[]{:S(2)}, u32[]{:S(2)}) collective-permute-start(bf16[640,512]{1,0:T(8,128)(2,1)} %prepare_sent.1), channel_id=1, source_target_pairs={{0,32},{1,33},{2,34},{3,35},{4,36},{5,37},{6,38},{7,39},{8,40},{9,... | collective-permute-start | bytes 1966088 | tf_op jit(solution)/shard_map/ppermute | solution.py:279
  10.9 0.0 copy-done
  10.9 0.0 copy-done.1
  10.9 0.0 copy-done.2
  10.9 0.0 copy-done.3
  10.9 0.8 prepare_kept.1.kept
  11.7 1.1 collective-permute-done.received
  12.8 0.4 pack.1
  13.2 1.9 %collective-permute-start.1 = (bf16[256,2048]{1,0:T(8,128)(2,1)S(1)}, bf16[256,2048]{1,0:T(8,128)(2,1)S(1)}, u32[]{:S(2)}, u32[]{:S(2)}) collective-permute-start(bf16[256,2048]{1,0:T(8,128)(2,1)S(1)} %get-tuple-element.7.own), channel_id=1, source_target_pairs={{0,1},{1,0},{2,3},{3,2},{4,5},{5,4},{6,7},{7,6},{8,9},{9,8},{10,11... | collective-permute-start | bytes 3145736 | tf_op jit(solution)/shard_map/ppermute | solution.py:282
  15.1 58.8 %all-gather.2 = s16[2048,1024]{1,0:T(8,128)(2,1)S(1)} all-gather(s16[128,1024]{1,0:T(8,128)(2,1)S(1)} %get-tuple-element.8), channel_id=2, replica_groups={{0,2,4,6,8,10,12,14,16,18,20,22,24,26,28,30},{1,3,5,7,9,11,13,15,17,19,..., dimensions={0}, use_global_device_ids=true | all-gather | bytes 4456448 | tf_op jit(solution)/shard_map/all_gather | solution.py:283
  73.9 0.0 collective-permute-done.1.partner
  73.9 5.7 %product.1 = s16[16,528,128]{2,1,0:T(8,128)(2,1)S(1)} custom-call(bf16[256,2048]{1,0:T(8,128)(2,1)S(1)} %get-tuple-element.7.own, bf16[256,2048]{1,0:T(8,128)(2,1)S(1)} %collective-permute-done.1.partner, s16[16,128,1024]{2,1,0:T(8,128)(2,1)S(1)} %bitcast.3), custom_call_target="tpu_custom_call" | custom-call | flops 4300000256 | bytes 9000000 | tf_op jit(solution)/shard_map/product/pallas_call | solution.py:219
  79.6 27.0 %all_to_all.5.arrived = s16[16,528,128]{2,1,0:T(8,128)(2,1)S(1)} all-to-all(s16[16,528,128]{2,1,0:T(8,128)(2,1)S(1)} %product.1), channel_id=1, replica_groups={{0,1,64,65,128,129,192,193,256,257,320,321,384,385,448,449},{2,3,66,67,..., dimensions={0} | all-to-all | bytes 4325376 | tf_op jit(solution)/shard_map/all_to_all | solution.py:284
  106.6 0.3 add_sent.1
  106.9 9.7 %collective-permute-start.2 = (f32[2,256,128]{2,1,0:T(8,128)S(1)}, f32[2,256,128]{2,1,0:T(8,128)S(1)}, u32[]{:S(2)}, u32[]{:S(2)}) collective-permute-start(f32[2,256,128]{2,1,0:T(8,128)S(1)} %add_sent.1), channel_id=1, source_target_pairs={{0,32},{1,33},{2,34},{3,35},{4,36},{5,37},{6,38},{7,39},{8,40},{9,... | collective-permute-start | bytes 786440 | tf_op jit(solution)/shard_map/ppermute | solution.py:285
  116.6 0.3 add_kept.1.keep
  116.9 0.8 collective-permute-done.2.received
  117.8 1.0 finish.1
Async XLA Ops:
  0.0 10.9 %copy-start = (bf16[2,2,256,512]{3,2,1,0:T(8,128)(2,1)S(1)}, bf16[2,2,256,512]{3,2,1,0:T(8,128)(2,1)}, u32[]{:S(2)}) copy-start(bf16[2,2,256,512]{3,2,1,0:T(8,128)(2,1)} %spectrum_in.3) | copy-start | bytes 3145732
  0.0 10.9 %copy-start.1 = (bf16[2,2,512,64]{2,3,1,0:T(8,128)(2,1)S(1)}, bf16[2,2,512,64]{2,3,1,0:T(8,128)(2,1)}, u32[]{:S(2)}) copy-start(bf16[2,2,512,64]{2,3,1,0:T(8,128)(2,1)} %param.5) | copy-start | bytes 786436
  0.0 10.9 %copy-start.2 = (s32[512]{0:T(512)S(1)}, s32[512]{0:T(512)}, u32[]{:S(2)}) copy-start(s32[512]{0:T(512)} %param.7) | copy-start | bytes 6148
  0.0 10.9 %copy-start.3 = (s32[8]{0:T(128)S(1)}, s32[8]{0:T(128)}, u32[]{:S(2)}) copy-start(s32[8]{0:T(128)} %centers_in.3) | copy-start | bytes 100
  2.1 10.7 %collective-permute-start = (bf16[640,512]{1,0:T(8,128)(2,1)}, bf16[640,512]{1,0:T(8,128)(2,1)S(1)}, u32[]{:S(2)}, u32[]{:S(2)}) collective-permute-start(bf16[640,512]{1,0:T(8,128)(2,1)} %prepare_sent.1), channel_id=1, source_target_pairs={{0,32},{1,33},{2,34},{3,35},{4,36},{5,37},{6,38},{7,39},{8,40},{9,... | collective-permute-start | bytes 1966088 | tf_op jit(solution)/shard_map/ppermute | solution.py:279
  13.2 60.7 %collective-permute-start.1 = (bf16[256,2048]{1,0:T(8,128)(2,1)S(1)}, bf16[256,2048]{1,0:T(8,128)(2,1)S(1)}, u32[]{:S(2)}, u32[]{:S(2)}) collective-permute-start(bf16[256,2048]{1,0:T(8,128)(2,1)S(1)} %get-tuple-element.7.own), channel_id=1, source_target_pairs={{0,1},{1,0},{2,3},{3,2},{4,5},{5,4},{6,7},{7,6},{8,9},{9,8},{10,11... | collective-permute-start | bytes 3145736 | tf_op jit(solution)/shard_map/ppermute | solution.py:282
  106.9 10.9 %collective-permute-start.2 = (f32[2,256,128]{2,1,0:T(8,128)S(1)}, f32[2,256,128]{2,1,0:T(8,128)S(1)}, u32[]{:S(2)}, u32[]{:S(2)}) collective-permute-start(f32[2,256,128]{2,1,0:T(8,128)S(1)} %add_sent.1), channel_id=1, source_target_pairs={{0,32},{1,33},{2,34},{3,35},{4,36},{5,37},{6,38},{7,39},{8,40},{9,... | collective-permute-start | bytes 786440 | tf_op jit(solution)/shard_map/ppermute | solution.py:285

commit v6 on v5

--- a/solution.py
+++ b/solution.py
@@ -253,12 +253,20 @@
     )(arrived)
 
 
-def finish_kernel(keep, received, out):
+def finish_kernel(keep, received, out, done, sems):
     core = core_index()
     low = lax.broadcasted_iota(jnp.int32, (1, LANES), 1) < COLS
-    for values, f in ((keep, core), (received, 1 - core)):
-        out[f, 0] = jnp.where(low, values[0], pltpu.roll(values[1], COLS, 1))
-        out[f, 1] = jnp.where(low, pltpu.roll(values[0], COLS, 1), values[1])
+    leaving = []
+    for which, (values, f) in enumerate(((keep, core), (received, 1 - core))):
+        for part in range(2):
+            if part == 0:
+                done[which, part] = jnp.where(low, values[0], pltpu.roll(values[1], COLS, 1))
+            else:
+                done[which, part] = jnp.where(low, pltpu.roll(values[0], COLS, 1), values[1])
+            leaving.append(pltpu.make_async_copy(done.at[which, part], out.at[f, part], sems.at[2 * which + part]))
+            leaving[-1].start()
+    for copy in leaving:
+        copy.wait()
 
 
 def finish(keep, received):
@@ -266,7 +274,8 @@
         finish_kernel,
         out_shape=jax.ShapeDtypeStruct((2, 2, ROWS, LANES), jnp.float32),
         in_specs=[vmem()] * 2,
-        out_specs=vmem(),
+        out_specs=anywhere(),
+        scratch_shapes=[pltpu.VMEM((2, 2, ROWS, LANES), jnp.float32), pltpu.SemaphoreType.DMA((4,))],
         compiler_params=params(),
         cost_estimate=pl.CostEstimate(flops=1_000_000, bytes_accessed=1_000_000, transcendentals=0),
         name="finish",

time: 119 us -> 119 us (level)
  no operation moved by 1% of the time
where the time goes in v6:
time: 119 us
  blocking collectives  85.8 us (72%)
  starting transfers between devices  20.4 us (17%)
  Pallas kernels  10.5 us (9%)
  waiting for transfers between devices  1.9 us (2%)
    all_gather x1, blocking collectives, shards(): gathered = lax.all_gather(code, AXES, axis_index_groups=ALONG_Z, axis=0)  58.8 us
    all_to_all x1, blocking collectives, shards(): lax.all_to_all(product(own, partner, gathered), AXES, 0, 0, axis_index_gr...  27 us
    ppermute x1, starting transfers between devices, shards(): received = lax.ppermute(add(True, arrived), AXES, CORE_PAIRS)  9.71 us
    ppermute x1, starting transfers between devices, shards(): received = lax.ppermute(prepare(True, *inputs), AXES, CORE_PAIRS)  8.78 us
    pallas_call x1, Pallas kernels, product(): pl.pallas_call(product_kernel, out_shape=jax.ShapeDtypeStruct((16, MSG, L...  5.75 us
    pallas_call x2, Pallas kernels, prepare(): pl.pallas_call(functools.partial(prepare_kernel, to_send), out_shape=jax....  2.86 us
  transfers between devices with their start and end apart: 3, of which 2 were waited for; matrix products, arithmetic and copies ran while one was open for 0% of the time, Pallas kernels for 1%

profile of v6, /device:TPU:1, one launch (start us, length us, event | category | flops | bytes accessed | tf_op | source)
XLA Modules:
  0.0 118.7 jit_solution(10808099342932811637)
XLA Ops:
  0.0 0.0 copy-start
  0.0 0.0 copy-start.1
  0.0 0.0 copy-start.2
  0.0 0.0 copy-start.3
  0.0 2.1 %prepare_sent.1 = bf16[640,512]{1,0:T(8,128)(2,1)} custom-call(bf16[2,2,256,512]{3,2,1,0:T(8,128)(2,1)} %spectrum_in.3, bf16[2,2,64,512]{3,2,1,0:T(8,128)(2,1)} %bitcast.4, s32[4,128]{1,0:T(4,128)} %bitcast.6, s32[8]{0:T(128)} %centers_in.3), custom_call_target="tpu_custom_call" | custom-call | flops 2000000000 | bytes 3000000 | tf_op jit(solution)/shard_map/prepare_sent/pallas_call | solution.py:111
  2.1 8.8 %collective-permute-start = (bf16[640,512]{1,0:T(8,128)(2,1)}, bf16[640,512]{1,0:T(8,128)(2,1)S(1)}, u32[]{:S(2)}, u32[]{:S(2)}) collective-permute-start(bf16[640,512]{1,0:T(8,128)(2,1)} %prepare_sent.1), channel_id=1, source_target_pairs={{0,32},{1,33},{2,34},{3,35},{4,36},{5,37},{6,38},{7,39},{8,40},{9,... | collective-permute-start | bytes 1966088 | tf_op jit(solution)/shard_map/ppermute | solution.py:288
  10.9 0.0 copy-done
  10.9 0.0 copy-done.1
  10.9 0.0 copy-done.2
  10.9 0.0 copy-done.3
  10.9 0.8 prepare_kept.1.kept
  11.7 1.1 collective-permute-done.received
  12.8 0.4 pack.1
  13.2 1.9 %collective-permute-start.1 = (bf16[256,2048]{1,0:T(8,128)(2,1)S(1)}, bf16[256,2048]{1,0:T(8,128)(2,1)S(1)}, u32[]{:S(2)}, u32[]{:S(2)}) collective-permute-start(bf16[256,2048]{1,0:T(8,128)(2,1)S(1)} %get-tuple-element.7.own), channel_id=1, source_target_pairs={{0,1},{1,0},{2,3},{3,2},{4,5},{5,4},{6,7},{7,6},{8,9},{9,8},{10,11... | collective-permute-start | bytes 3145736 | tf_op jit(solution)/shard_map/ppermute | solution.py:291
  15.1 58.8 %all-gather.2 = s16[2048,1024]{1,0:T(8,128)(2,1)S(1)} all-gather(s16[128,1024]{1,0:T(8,128)(2,1)S(1)} %get-tuple-element.8), channel_id=2, replica_groups={{0,2,4,6,8,10,12,14,16,18,20,22,24,26,28,30},{1,3,5,7,9,11,13,15,17,19,..., dimensions={0}, use_global_device_ids=true | all-gather | bytes 4456448 | tf_op jit(solution)/shard_map/all_gather | solution.py:292
  73.9 0.0 collective-permute-done.1.partner
  73.9 5.7 %product.1 = s16[16,528,128]{2,1,0:T(8,128)(2,1)S(1)} custom-call(bf16[256,2048]{1,0:T(8,128)(2,1)S(1)} %get-tuple-element.7.own, bf16[256,2048]{1,0:T(8,128)(2,1)S(1)} %collective-permute-done.1.partner, s16[16,128,1024]{2,1,0:T(8,128)(2,1)S(1)} %bitcast.3), custom_call_target="tpu_custom_call" | custom-call | flops 4300000256 | bytes 9000000 | tf_op jit(solution)/shard_map/product/pallas_call | solution.py:219
  79.6 27.0 %all_to_all.5.arrived = s16[16,528,128]{2,1,0:T(8,128)(2,1)S(1)} all-to-all(s16[16,528,128]{2,1,0:T(8,128)(2,1)S(1)} %product.1), channel_id=1, replica_groups={{0,1,64,65,128,129,192,193,256,257,320,321,384,385,448,449},{2,3,66,67,..., dimensions={0} | all-to-all | bytes 4325376 | tf_op jit(solution)/shard_map/all_to_all | solution.py:293
  106.6 0.3 add_sent.1
  106.9 9.7 %collective-permute-start.2 = (f32[2,256,128]{2,1,0:T(8,128)S(1)}, f32[2,256,128]{2,1,0:T(8,128)S(1)}, u32[]{:S(2)}, u32[]{:S(2)}) collective-permute-start(f32[2,256,128]{2,1,0:T(8,128)S(1)} %add_sent.1), channel_id=1, source_target_pairs={{0,32},{1,33},{2,34},{3,35},{4,36},{5,37},{6,38},{7,39},{8,40},{9,... | collective-permute-start | bytes 786440 | tf_op jit(solution)/shard_map/ppermute | solution.py:294
  116.6 0.3 add_kept.1.keep
  116.9 0.8 collective-permute-done.2.received
  117.8 0.9 finish.1
Async XLA Ops:
  0.0 10.9 %copy-start = (bf16[2,2,256,512]{3,2,1,0:T(8,128)(2,1)S(1)}, bf16[2,2,256,512]{3,2,1,0:T(8,128)(2,1)}, u32[]{:S(2)}) copy-start(bf16[2,2,256,512]{3,2,1,0:T(8,128)(2,1)} %spectrum_in.3) | copy-start | bytes 3145732
  0.0 10.9 %copy-start.1 = (bf16[2,2,512,64]{2,3,1,0:T(8,128)(2,1)S(1)}, bf16[2,2,512,64]{2,3,1,0:T(8,128)(2,1)}, u32[]{:S(2)}) copy-start(bf16[2,2,512,64]{2,3,1,0:T(8,128)(2,1)} %param.5) | copy-start | bytes 786436
  0.0 10.9 %copy-start.2 = (s32[512]{0:T(512)S(1)}, s32[512]{0:T(512)}, u32[]{:S(2)}) copy-start(s32[512]{0:T(512)} %param.7) | copy-start | bytes 6148
  0.0 10.9 %copy-start.3 = (s32[8]{0:T(128)S(1)}, s32[8]{0:T(128)}, u32[]{:S(2)}) copy-start(s32[8]{0:T(128)} %centers_in.3) | copy-start | bytes 100
  2.1 10.7 %collective-permute-start = (bf16[640,512]{1,0:T(8,128)(2,1)}, bf16[640,512]{1,0:T(8,128)(2,1)S(1)}, u32[]{:S(2)}, u32[]{:S(2)}) collective-permute-start(bf16[640,512]{1,0:T(8,128)(2,1)} %prepare_sent.1), channel_id=1, source_target_pairs={{0,32},{1,33},{2,34},{3,35},{4,36},{5,37},{6,38},{7,39},{8,40},{9,... | collective-permute-start | bytes 1966088 | tf_op jit(solution)/shard_map/ppermute | solution.py:288
  13.2 60.7 %collective-permute-start.1 = (bf16[256,2048]{1,0:T(8,128)(2,1)S(1)}, bf16[256,2048]{1,0:T(8,128)(2,1)S(1)}, u32[]{:S(2)}, u32[]{:S(2)}) collective-permute-start(bf16[256,2048]{1,0:T(8,128)(2,1)S(1)} %get-tuple-element.7.own), channel_id=1, source_target_pairs={{0,1},{1,0},{2,3},{3,2},{4,5},{5,4},{6,7},{7,6},{8,9},{9,8},{10,11... | collective-permute-start | bytes 3145736 | tf_op jit(solution)/shard_map/ppermute | solution.py:291
  106.9 10.9 %collective-permute-start.2 = (f32[2,256,128]{2,1,0:T(8,128)S(1)}, f32[2,256,128]{2,1,0:T(8,128)S(1)}, u32[]{:S(2)}, u32[]{:S(2)}) collective-permute-start(f32[2,256,128]{2,1,0:T(8,128)S(1)} %add_sent.1), channel_id=1, source_target_pairs={{0,32},{1,33},{2,34},{3,35},{4,36},{5,37},{6,38},{7,39},{8,40},{9,... | collective-permute-start | bytes 786440 | tf_op jit(solution)/shard_map/ppermute | solution.py:294
